TPU v7x, 128 devices: a whole 4x4x4 slice. The times are simulated.
128 devices in a mesh: section: 8 (over y_hi, x), seq: 16 (over y_lo, z, core).
Axes of the slice: x: 4, y: 4 (y_hi: 2, y_lo: 2; y = y_hi * 2 + y_lo), z: 4, core: 2. Of those that a mesh axis runs over, the one named last changes fastest.
Arguments:
- video: bfloat16 [8, 2048, 3072], P('section', 'seq'), may hold values from -6 to 6
- text: bfloat16 [8, 128, 3072], P('section', 'seq'), may hold values from -6 to 6
- prompt_len: int32 [8], P('section'), may hold values from 1 to 128, as said below
- modulation: float32 [8, 3, 3072], P('section'), may hold values from -3 to 3
- q_gain: float32 [128], replicated, may hold values from 0.5 to 2
- k_gain: float32 [128], replicated, may hold values from 0.5 to 2
- w_qkv: bfloat16 [3072, 3, 2048], P(None, None, 'seq'), may hold values from -0.109375 to 0.109375
- w_out: bfloat16 [2048, 3072], replicated, may hold values from -0.125 to 0.125
- cot_video: bfloat16 [8, 2048, 3072], P('section', 'seq'), may hold values from -6 to 6
- cot_text: bfloat16 [8, 128, 3072], P('section', 'seq'), may hold values from -6 to 6
Outputs:
- video_out: bfloat16 [8, 2048, 3072], P('section', 'seq')
- text_out: bfloat16 [8, 128, 3072], P('section', 'seq')
- grad_video: bfloat16 [8, 2048, 3072], P('section', 'seq')
- grad_text: bfloat16 [8, 128, 3072], P('section', 'seq')
- grad_modulation: float32 [8, 3, 3072], P('section')
- grad_wqkv: float32 [3072, 3, 2048], P('section', None, 'seq')
- grad_gains: float32 [2, 128], replicated
Inputs may be any that keep to these rules, and one draw needn't show every extreme that they name: `prompt_len`: some sample uses all 128 text rows.
All inputs are finite; a program needn't handle non-finite values.
Results may differ from a plain program's by a relative error of at most 0.019.
Values may be sent and summed in bfloat16 or wider, within the bound.
No kernel may reach another device: no remote copies, remote signals or barrier semaphores. Data moves between devices by JAX's collectives and lax.ppermute only.
A program may use at most 192 MiB of HBM per device.

v0:
```python
import functools
import jax
import jax.numpy as jnp
from jax import lax
from jax.experimental import pallas as pl
from jax.experimental.pallas import tpu as pltpu
from jax.sharding import Mesh
from jax.sharding import PartitionSpec as P

BF = jnp.bfloat16
F = jnp.float32
HD = 128
SEQ = ("y", "z", "core")
SECTION = ("yh", "x")
EVERY = SECTION + SEQ
NT = (((1,), (1,)), ((), ()))
TN = (((0,), (0,)), ((), ()))
PLACES = [(0, 0), (1, 0), (0, -1), (0, 1), (0, 2), (1, -1), (1, 1), (1, 2)]


def shape(dims, kind=BF):
    return jax.ShapeDtypeStruct(dims, kind)


def whole(dims):
    return pl.BlockSpec(dims, lambda *_: (0,) * len(dims))


def call(kernel, outs, mib=48, us=0, **more):
    return pl.pallas_call(
        kernel,
        out_shape=outs,
        compiler_params=pltpu.CompilerParams(vmem_limit_bytes=mib * 2**20),
        cost_estimate=pl.CostEstimate(flops=int(us * 1.1e9) + 1, bytes_accessed=1, transcendentals=0),
        **more,
    )


def side_by_side(*refs):
    return jnp.concatenate([ref[j] for ref in refs for j in range(3)], axis=1)


def layer_norm(x):
    center = x - jnp.mean(x, axis=-1, keepdims=True)
    rstd = lax.rsqrt(jnp.mean(center * center, axis=-1, keepdims=True) + 1e-06)
    return center * rstd, rstd


def modulate_kernel(video_ref, text_ref, mod_ref, h_ref):
    shift, scale = mod_ref[0:1, :], 1.0 + mod_ref[1:2, :]
    vrows = video_ref.shape[0]
    for i in range(0, vrows, 16):
        normed, _ = layer_norm(video_ref[i : i + 16, :].astype(F))
        h_ref[i : i + 16, :] = (normed * scale + shift).astype(BF)
    normed, _ = layer_norm(text_ref[...].astype(F))
    h_ref[vrows:, :] = (normed * scale + shift).astype(BF)


def split_kernel(cut, y_ref, a_ref, b_ref, yt_ref, yl_ref, at_ref, bl_ref, m_ref):
    part = y_ref.shape[0] - cut
    yt_ref[...] = y_ref[:cut, :]
    yl_ref[...] = y_ref[cut:, :]
    at_ref[...] = a_ref[:cut, :]
    bl_ref[...] = b_ref[cut:, :]
    m_ref[:part, :] = a_ref[cut:, :]
    m_ref[part:, :] = b_ref[:cut, :]


def qkv_kernel(pieces, *refs):
    own_w, sib_w = refs[pieces : pieces + 2]
    h_ref, own_ref, sib_ref, acc = refs[pieces + 2 :]
    h = jnp.concatenate([ref[...] for ref in refs[:pieces]], axis=0)
    h_ref[...] = h
    w = side_by_side(own_w, sib_w)
    got = jnp.dot(h, w, preferred_element_type=F)
    step = pl.program_id(0)

    @pl.when(step == 0)
    def _():
        acc[...] = got

    @pl.when(step > 0)
    def _():
        acc[...] += got

    @pl.when(step == pl.num_programs(0) - 1)
    def _():
        cols = own_ref.shape[1]
        own_ref[...] = acc[:, :cols].astype(BF)
        sib_ref[...] = acc[:, cols:].astype(BF)


def d_attn_kernel(video_ref, text_ref, gate_ref, w_ref, out_ref, d_out):
    @pl.when(pl.program_id(0) == 0)
    def _():
        vrows = video_ref.shape[0]
        d_out[0:vrows, :] = (video_ref[...].astype(F) * gate_ref[...]).astype(BF)
        d_out[vrows:, :] = (text_ref[...].astype(F) * gate_ref[...]).astype(BF)

    got = lax.dot_general(d_out[...], w_ref[...], NT, preferred_element_type=F)
    for j in range(out_ref.shape[0]):
        out_ref[j] = got[:, j * HD : (j + 1) * HD].astype(BF)


def out_kernel(attn_ref, w_ref, video_ref, text_ref, dv_ref, dt_ref, gate_ref, ov_ref, ot_ref, dg_ref, tok):
    rows = tok.shape[0]

    @pl.when(pl.program_id(0) == 0)
    def _():
        for j in range(attn_ref.shape[0]):
            tok[:, j * HD : (j + 1) * HD] = attn_ref[j, 0:rows, :]

    out = jnp.dot(tok[...], w_ref[...], preferred_element_type=F)
    vrows = video_ref.shape[0]
    top, low = out[:vrows], out[vrows:]
    gate = gate_ref[...]
    ov_ref[...] = (video_ref[...].astype(F) + gate * top).astype(BF)
    ot_ref[...] = (text_ref[...].astype(F) + gate * low).astype(BF)
    dg_ref[...] = jnp.sum(dv_ref[...].astype(F) * top, axis=0, keepdims=True) + jnp.sum(
        dt_ref[...].astype(F) * low, axis=0, keepdims=True
    )


def far_kernel(cut, own_ref, sib_ref, wo_ref, ws_ref, yct_ref, ycl_ref, m1_ref, m2_ref, m_ref):
    d = jnp.concatenate([own_ref[...], sib_ref[...]], axis=1)
    w = side_by_side(wo_ref, ws_ref)
    got = lax.dot_general(d, w, NT, preferred_element_type=F)
    rows = got.shape[0] // 4
    c, ya, yb, yc = (got[i * rows : (i + 1) * rows] for i in range(4))
    yct_ref[...] = yc[:cut].astype(BF)
    ycl_ref[...] = yc[cut:].astype(BF)
    m1_ref[...] = jnp.concatenate([ya[:cut], c[:cut]], axis=0).astype(BF)
    m2_ref[...] = jnp.concatenate([yb[cut:], c[cut:]], axis=0).astype(BF)
    m_ref[...] = jnp.concatenate([ya[cut:], yb[:cut]], axis=0).astype(BF)


def add_kernel(base_ref, got_ref, out_ref):
    n = got_ref.shape[0]
    out_ref[:n, :] = (base_ref[:n, :].astype(F) + got_ref[...].astype(F)).astype(BF)
    out_ref[n:, :] = base_ref[n:, :]


def sums_kernel(cut, y_ref, a_ref, b_ref, r1_ref, r2_ref, r3_ref, oy_ref, oa_ref, ob_ref):
    part = y_ref.shape[0] - cut
    r1, r2, r3 = (ref[...].astype(F) for ref in (r1_ref, r2_ref, r3_ref))
    parts = (
        (y_ref, oy_ref, r1[:cut], r2[:part]),
        (a_ref, oa_ref, r1[cut:], r3[:part]),
        (b_ref, ob_ref, r3[part:], r2[part:]),
    )
    for ref, out, top, low in parts:
        out[...] = (ref[...].astype(F) + jnp.concatenate([top, low], axis=0)).astype(BF)


def near_kernel(own_ref, sib_ref, wo_ref, ws_ref, o_ref, y_ref, a_ref, b_ref):
    d = jnp.concatenate([own_ref[...], sib_ref[...]], axis=1)
    w = side_by_side(wo_ref, ws_ref)
    got = lax.dot_general(d, w, NT, preferred_element_type=F)
    rows = got.shape[0] // 4
    for i, ref in enumerate((o_ref, y_ref, a_ref, b_ref)):
        ref[...] = got[i * rows : (i + 1) * rows].astype(BF)


def grad_w_kernel(place_ref, one_ref, two_ref, own_ref, sib_ref, own_out, sib_out):
    h = jnp.concatenate([one_ref[...], two_ref[...]], axis=0)
    d = jnp.concatenate([own_ref[...], sib_ref[...]], axis=1)
    got = lax.dot_general(h, d, TN, preferred_element_type=F)
    wide, cols = own_out.shape[3], own_ref.shape[1]
    count = h.shape[1] // wide
    for i in range(count):
        at = (lax.rem(pl.program_id(0) * count, 4) + i - place_ref[0]) % 4
        for j in range(3):
            piece = got[i * wide : (i + 1) * wide]
            own_out[at, 0, j] = piece[:, j * HD : (j + 1) * HD].astype(BF)
            sib_out[at, 0, j] = piece[:, cols + j * HD : cols + (j + 1) * HD].astype(BF)


def gain_terms(values):
    high = values.astype(BF).astype(F)
    mid = (values - high).astype(BF).astype(F)
    low = values - high - mid
    pad = jnp.zeros((2, HD), F)
    return jnp.concatenate([high, mid, low, pad], axis=0).astype(BF)


def gain_value(terms):
    terms = terms.astype(F)
    return terms[0:2] + terms[2:4] + terms[4:6]


def both(own_ref, got_ref, k):
    total = own_ref[0, k].astype(F) + got_ref[0, k].astype(F)
    return total.reshape(total.shape[0] * total.shape[1], total.shape[2])


def far_section_kernel(own_ref, got_ref, attn_ref, f0_ref, f1_ref, gain_ref):
    flat = f0_ref.shape[0] - 8
    gains = gain_value(jnp.sum(attn_ref[...].astype(F), axis=0))
    for k, ref in enumerate((f0_ref, f1_ref)):
        ref[0:flat, :] = both(own_ref, got_ref, k).astype(BF)
        ref[flat:, :] = gain_terms(gains)
    gain_ref[...] = gains


def near_section_kernel(ao_ref, ag_ref, bo_ref, bg_ref, ga_ref, gb_ref, gain_ref, sa_ref, sb_ref, sum_ref):
    flat = ga_ref.shape[0] - 8
    sa_ref[0:flat, :] = both(ao_ref, ag_ref, 0).astype(BF)
    sa_ref[flat : 2 * flat, :] = (both(ao_ref, ag_ref, 1) + ga_ref[0:flat, :].astype(F)).astype(BF)
    sa_ref[2 * flat :, :] = ga_ref[flat:, :]
    sb_ref[0:flat, :] = (both(bo_ref, bg_ref, 0) + gb_ref[0:flat, :].astype(F)).astype(BF)
    sb_ref[flat:, :] = both(bo_ref, bg_ref, 1).astype(BF)
    sum_ref[...] = gain_ref[...] + gain_value(ga_ref[flat:, :]) + gain_value(gb_ref[flat:, :])


def own_section_kernel(own_ref, got_ref, a_ref, b_ref, gain_ref, keep_ref, give_ref, sum_ref):
    flat = keep_ref.shape[0]
    keep = both(own_ref, got_ref, 0)
    give = both(own_ref, got_ref, 1)
    keep_ref[...] = keep + a_ref[0:flat, :].astype(F) + b_ref[0:flat, :].astype(F)
    give += a_ref[flat : 2 * flat, :].astype(F) + b_ref[flat : 2 * flat, :].astype(F)
    give_ref[0:flat, :] = give.astype(BF)
    gains = gain_ref[...] + gain_value(a_ref[2 * flat :, :])
    give_ref[flat:, :] = gain_terms(gains)
    sum_ref[...] = gains


def tail_kernel(o_ref, ra_ref, rb_ref, ry_ref, video_ref, text_ref, dv_ref, dt_ref, mod_ref, dg_ref, gv_ref, gt_ref, m_ref):
    scale = 1.0 + mod_ref[1:2, :]
    vrows = video_ref.shape[0]
    first = jnp.zeros((8, scale.shape[1]), F)
    second = first
    everything = lambda at, n: (
        o_ref[at : at + n, :].astype(F)
        + ra_ref[at : at + n, :].astype(F)
        + rb_ref[at : at + n, :].astype(F)
        + ry_ref[at : at + n, :].astype(F)
    )
    fold = lambda v: jnp.sum(v.reshape(v.shape[0] // 8, 8, v.shape[1]), axis=0)
    pieces = [(i, 16, video_ref, dv_ref, gv_ref, i) for i in range(0, vrows, 16)]
    pieces.append((vrows, text_ref.shape[0], text_ref, dt_ref, gt_ref, 0))
    for at, n, x_ref, dy_ref, g_ref, lo in pieces:
        d_h = everything(at, n)
        normed, rstd = layer_norm(x_ref[lo : lo + n, :].astype(F))
        t = d_h * scale
        back = rstd * (
            t
            - jnp.mean(t, axis=-1, keepdims=True)
            - normed * jnp.mean(t * normed, axis=-1, keepdims=True)
        )
        g_ref[lo : lo + n, :] = (dy_ref[lo : lo + n, :].astype(F) + back).astype(BF)
        first += fold(d_h)
        second += fold(d_h * normed)
    rows = [jnp.sum(v, axis=0, keepdims=True) for v in (first, second)] + [dg_ref[...]]
    m = jnp.concatenate(rows, axis=0).astype(BF)
    m_ref[...] = jnp.broadcast_to(m[None], m_ref.shape)


def rms(x):
    r = lax.rsqrt(jnp.mean(x * x, axis=-1, keepdims=True) + 1e-6)
    return x * r, r


def rms_back(t, xh, r):
    return r * (t - xh * jnp.mean(t * xh, axis=-1, keepdims=True))


def attn_kernel(
    rows, order_ref, q1_ref, q2_ref, s1_ref, s2_ref, bias_ref, do_ref, gq_ref, gk_ref,
    attn_ref, own_ref, give_ref, q_s, kn_s, v_s, dq_s, dk_s, dv_s, gain_s,
):
    block = q1_ref.shape[0]
    parts = (q1_ref, q2_ref, s1_ref, s2_ref)
    outs = ((own_ref, 0), (own_ref, block), (give_ref, 0), (give_ref, block))
    per = block // rows
    scale = HD**-0.5
    step = pl.program_id(0)
    gq, gk = gq_ref[...], gk_ref[...]

    @pl.when(step == 0)
    def _():
        for i, ref in enumerate(parts):
            at = slice(i * block, (i + 1) * block)
            q_s[at, :] = ref[:, 0:HD]
            xh, _ = rms(ref[:, HD : 2 * HD].astype(F))
            kn_s[at, :] = (xh * gk).astype(BF)
            v_s[at, :] = ref[:, 2 * HD : 3 * HD]
        dk_s[...] = jnp.zeros_like(dk_s)
        dv_s[...] = jnp.zeros_like(dv_s)
        gain_s[...] = jnp.zeros_like(gain_s)

    here = pl.ds(pl.multiple_of(step * block, 16), block)
    xh, r = rms(q_s[here, :].astype(F))
    qn = (xh * (gq * scale)).astype(BF)
    s = lax.dot_general(qn, kn_s[...], NT, preferred_element_type=F) + bias_ref[...]
    e = jnp.exp(s)
    linv = 1.0 / jnp.sum(e, axis=-1, keepdims=True)
    eb = e.astype(BF)
    o = jnp.dot(eb, v_s[...], preferred_element_type=F) * linv
    do = jnp.concatenate(
        [do_ref[order_ref[step * per + j]].astype(F) for j in range(per)], axis=0
    )
    for j in range(per):
        attn_ref[order_ref[step * per + j], 0:rows, :] = o[j * rows : (j + 1) * rows].astype(BF)
    dn = do * linv
    dnb = dn.astype(BF)
    delta = jnp.sum(dn * o, axis=-1, keepdims=True)
    dp = lax.dot_general(dnb, v_s[...], NT, preferred_element_type=F)
    ds = (e * (dp - delta)).astype(BF)
    dq = jnp.dot(ds, kn_s[...], preferred_element_type=F)
    dk_s[...] += lax.dot_general(ds, qn, TN, preferred_element_type=F)
    dv_s[...] += lax.dot_general(eb, dnb, TN, preferred_element_type=F)
    gain_s[0:1, :] += jnp.sum(dq * xh, axis=0, keepdims=True) * scale
    dq_s[here, :] = rms_back(dq * (gq * scale), xh, r).astype(BF)

    @pl.when(step == 3)
    def _():
        for i, ref in enumerate(parts):
            out, at = outs[i]
            out[at : at + block, 0:HD] = dq_s[i * block : (i + 1) * block, :]
            xh, r = rms(ref[:, HD : 2 * HD].astype(F))
            dk = dk_s[i * block : (i + 1) * block, :]
            gain_s[1:2, :] += jnp.sum(dk * xh, axis=0, keepdims=True)
            out[at : at + block, HD : 2 * HD] = rms_back(dk * gk, xh, r).astype(BF)
            out[at : at + block, 2 * HD :] = dv_s[i * block : (i + 1) * block, :].astype(BF)
        gains = gain_s[...]
        high = gains.astype(BF).astype(F)
        low = (gains - high).astype(BF).astype(F)
        rest = gains - high - low
        tail = jnp.concatenate([high[0:2], low[0:2], rest[0:2], jnp.zeros((2, HD), F)], axis=0)
        attn_ref[:, rows:, :] = jnp.broadcast_to(tail.astype(BF)[None], (attn_ref.shape[0], 8, HD))


def ring(values, axis, distance):
    size = lax.axis_size(axis)
    return lax.ppermute(values, axis, [(i, (i + distance) % size) for i in range(size)])


def tie(values, *after):
    return lax.optimization_barrier((values, *after))[0]


def per_device(
    video, text, prompt_len, modulation, q_gain, k_gain, w_qkv, w_out, cot_video, cot_text
):
    video, text, cot_video, cot_text, modulation = (
        a[0] for a in (video, text, cot_video, cot_text, modulation)
    )
    vrows, trows = video.shape[0], text.shape[0]
    rows, width = vrows + trows, video.shape[1]
    heads = w_out.shape[0] // HD
    cols = 3 * HD
    yi, zi, ci = (lax.axis_index(a) for a in SEQ)
    zp = functools.partial(ring, axis="z", distance=1)
    zm = functools.partial(ring, axis="z", distance=-1)
    yy = functools.partial(ring, axis="y", distance=1)
    cc = functools.partial(ring, axis="core", distance=1)
    gate = modulation[2:3]
    cut = 64
    part = rows - cut

    h = call(modulate_kernel, shape((rows, width)))(video, text, modulation)
    w_own = jnp.transpose(w_qkv, (1, 0, 2))
    step = 2 * HD
    per = 4

    w_sib = cc(w_own)
    h_a, h_b, h_y = zp(h), zm(h), yy(h)
    d_attn = call(
        d_attn_kernel,
        shape((heads, rows, HD)),
        grid=(2 * per,),
        in_specs=[
            whole((vrows, width)),
            whole((trows, width)),
            whole((1, width)),
            pl.BlockSpec((step, width), lambda i: (i, 0)),
        ],
        out_specs=pl.BlockSpec((step // HD, rows, HD), lambda i: (i, 0, 0)),
        scratch_shapes=[pltpu.VMEM((rows, width), BF)],
    )(cot_video, cot_text, tie(gate, h, w_sib), w_out)
    y_t, y_l, a_t, b_l, m_ab = call(
        functools.partial(split_kernel, cut), tuple(shape((k, width)) for k in (cut, part, cut, part, rows))
    )(tie(h_y, d_attn), h_a, h_b)
    ya_t, yb_l = zp(y_t), zm(y_l)
    c_t, c_l = zp(a_t), zm(b_l)
    m_ab = yy(m_ab)
    n = len(PLACES) * rows
    block = n // 2
    strip = 1024

    def project(us, *parts):
        return call(
            functools.partial(qkv_kernel, len(parts)),
            (shape((block, width)), shape((block, cols)), shape((block, cols))),
            mib=56,
            us=us,
            grid=(width // strip,),
            in_specs=[pl.BlockSpec((k.shape[0], strip), lambda i: (0, i)) for k in parts]
            + [pl.BlockSpec((3, strip, HD), lambda i: (0, i, 0))] * 2,
            out_specs=[
                pl.BlockSpec((block, strip), lambda i: (0, i)),
                whole((block, cols)),
                whole((block, cols)),
            ],
            scratch_shapes=[pltpu.VMEM((block, 2 * cols), F)],
        )(*parts, w_own, w_sib)

    h_one, own_one, sib_one = project(0, h, h_y, h_a, h_b)
    yc_t, yc_l = zp(tie(ya_t, own_one)), zm(tie(yb_l, own_one))
    d_heads = lax.all_to_all(
        tie(d_attn, yc_t, yc_l), SEQ, split_axis=0, concat_axis=0, tiled=True
    )
    h_two, own_two, sib_two = project(0, c_t, c_l, ya_t, m_ab, yb_l, yc_t, yc_l)
    sib_two = cc(sib_two)
    sib_one = cc(tie(sib_one, own_two))

    order = jnp.stack(
        [(((yi + a) % 2) * 4 + (zi + b) % 4) * 2 + (ci + k) % 2 for k in (0, 1) for a, b in PLACES]
    ).astype(jnp.int32)
    inner = jnp.arange(rows, dtype=jnp.int32)[None, :]
    valid = (inner < vrows) | (order[:, None] * trows + inner - vrows < prompt_len[0])
    bias = jnp.where(valid, 0.0, -1e30).astype(F).reshape(1, 2 * n)

    attn, d_own, d_give = call(
        functools.partial(attn_kernel, rows),
        (shape((heads, rows + 8, HD)), shape((n, cols)), shape((n, cols))),
        mib=56,
        grid_spec=pltpu.PrefetchScalarGridSpec(
            num_scalar_prefetch=1,
            grid=(4,),
            in_specs=[whole(a) for a in ((block, cols),) * 4]
            + [whole((1, 2 * n)), whole((heads, rows, HD)), whole((1, HD)), whole((1, HD))],
            out_specs=[whole((heads, rows + 8, HD)), whole((n, cols)), whole((n, cols))],
            scratch_shapes=[
                pltpu.VMEM((2 * n, HD), BF),
                pltpu.VMEM((2 * n, HD), BF),
                pltpu.VMEM((2 * n, HD), BF),
                pltpu.VMEM((2 * n, HD), BF),
                pltpu.VMEM((2 * n, HD), F),
                pltpu.VMEM((2 * n, HD), F),
                pltpu.VMEM((8, HD), F),
            ],
        ),
    )(order, own_one, own_two, sib_one, sib_two, bias, d_heads, q_gain[None], k_gain[None])

    d_sib = cc(d_give)

    xi, hi = lax.axis_index("x"), lax.axis_index("yh")
    wide = width // 8
    here = jnp.stack([xi - 4, hi - 2]).astype(jnp.int32)

    attn_tok = lax.all_to_all(attn, SEQ, split_axis=0, concat_axis=0, tiled=True)
    strips = lambda count: pl.BlockSpec((count, strip), lambda i: (0, i))
    sizes = (cut, part, 2 * cut, 2 * part, rows)
    half_specs = lambda at: [
        pl.BlockSpec((block, cols), lambda i: (at, 0)),
        pl.BlockSpec((block, cols), lambda i: (at, 0)),
        pl.BlockSpec((3, strip, HD), lambda i: (0, i, 0)),
        pl.BlockSpec((3, strip, HD), lambda i: (0, i, 0)),
    ]
    work = dict(grid=(width // strip,), mib=56)
    yc_t, yc_l, m_1, m_2, m_3 = call(
        functools.partial(far_kernel, cut),
        tuple(shape((k, width)) for k in sizes),
        in_specs=half_specs(1),
        out_specs=[strips(k) for k in sizes],
        **work,
    )(d_own, d_sib, w_own, w_sib)
    r_ya, r_yb = zm(yc_t), zp(yc_l)
    r_3 = yy(m_3)
    g_own, g_sib = call(
        grad_w_kernel,
        (shape((4, 2, 3, wide, HD)),) * 2,
        us=12,
        mib=56,
        grid_spec=pltpu.PrefetchScalarGridSpec(
            num_scalar_prefetch=1,
            grid=(4,),
            in_specs=[pl.BlockSpec((block, 2 * wide), lambda i, p: (0, i))] * 2
            + [whole((n, cols))] * 2,
            out_specs=[
                pl.BlockSpec((4, 1, 3, wide, HD), lambda i, p: (0, (i // 2 - p[1]) % 2, 0, 0, 0))
            ]
            * 2,
        ),
    )(tie(here, m_3), h_one, h_two, d_own, d_sib)

    p_o, p_y, p_a, p_b = call(
        near_kernel,
        (shape((rows, width)),) * 4,
        in_specs=half_specs(0),
        out_specs=[strips(rows)] * 4,
        us=30,
        **work,
    )(tie(d_own, m_3), d_sib, w_own, w_sib)

    thirds = lambda count: pl.BlockSpec((count, width // 3), lambda i: (0, i))

    def add(base, got):
        return call(
            add_kernel,
            shape(base.shape),
            grid=(3,),
            in_specs=[thirds(base.shape[0]), thirds(got.shape[0])],
            out_specs=thirds(base.shape[0]),
        )(base, got)

    r_1, r_2 = zm(add(tie(m_1, g_own), r_ya)), zp(add(tie(m_2, g_own), r_yb))
    g_got = cc(g_sib)
    flat = 3 * wide
    pick = lambda r: [pl.BlockSpec((1, 2, 3, wide, HD), lambda i: (r, 0, 0, 0, 0))] * 2
    two = shape((2, HD), F)
    far_0, far_1, gains = call(
        far_section_kernel,
        (shape((flat + 8, HD)), shape((flat + 8, HD)), two),
        grid=(1,),
        in_specs=pick(2) + [pl.BlockSpec((heads, 8, HD), lambda i: (0, rows // 8, 0))],
        out_specs=[whole((flat + 8, HD)), whole((flat + 8, HD)), whole((2, HD))],
    )(g_own, g_got, tie(attn_tok, p_o))
    got_b, got_a = ring(far_0, "x", -1), ring(far_1, "x", 1)
    p_y, p_a, p_b = call(
        functools.partial(sums_kernel, cut),
        (shape((rows, width)),) * 3,
        grid=(3,),
        in_specs=[thirds(k) for k in (rows, rows, rows, 2 * cut, 2 * part, rows)],
        out_specs=[thirds(rows)] * 3,
    )(
        tie(p_y, far_0, far_1), p_a, p_b, r_1, r_2, r_3
    )
    last_a, last_b, last_y = zm(p_a), zp(p_b), yy(p_y)

    send_a, send_b, gains = call(
        near_section_kernel,
        (shape((2 * flat + 8, HD)), shape((2 * flat, HD)), two),
        grid=(1,),
        in_specs=pick(1) + pick(3) + [whole((flat + 8, HD))] * 2 + [whole((2, HD))],
        out_specs=[whole((2 * flat + 8, HD)), whole((2 * flat, HD)), whole((2, HD))],
    )(g_own, g_got, g_own, g_got, got_a, got_b, gains)
    back_a, back_b = ring(send_a, "x", 1), ring(send_b, "x", -1)
    keep, give, gains = call(
        own_section_kernel,
        (shape((flat, HD), F), shape((flat + 8, HD)), two),
        grid=(1,),
        in_specs=pick(0) + [whole((2 * flat + 8, HD)), whole((2 * flat, HD)), whole((2, HD))],
        out_specs=[whole((flat, HD)), whole((flat + 8, HD)), whole((2, HD))],
    )(g_own, g_got, back_a, back_b, gains)
    got = ring(give, "yh", 1)
    grad_w = (keep + got[:flat].astype(F)).reshape(3, wide, HD)
    grad_w = jnp.transpose(grad_w, (1, 0, 2))
    last = got[flat:].astype(F)
    grad_gain = gains + last[0:2] + last[2:4] + last[4:6]

    out_video, out_text, d_gate = call(
        out_kernel,
        (shape((vrows, width)), shape((trows, width)), shape((1, width), F)),
        us=8,
        grid=(width // strip,),
        mib=56,
        in_specs=[
            whole((heads, rows + 8, HD)),
            pl.BlockSpec((heads * HD, strip), lambda i: (0, i)),
        ]
        + [strips(k) for k in (vrows, trows, vrows, trows, 1)],
        out_specs=[strips(k) for k in (vrows, trows, 1)],
        scratch_shapes=[pltpu.VMEM((rows, heads * HD), BF)],
    )(tie(attn_tok, p_y, send_a, send_b), w_out, video, text, cot_video, cot_text, gate)

    grad_video, grad_text, wide_mod = call(
        tail_kernel,
        (shape((vrows, width)), shape((trows, width)), shape((heads, 3, width))),
    )(tie(p_o, give), last_a, last_b, last_y, video, text, cot_video, cot_text, modulation, d_gate)
    grad_mod = jnp.sum(
        lax.all_to_all(wide_mod, SEQ, split_axis=0, concat_axis=0, tiled=True).astype(F), axis=0
    )
    return (
        out_video[None],
        out_text[None],
        grad_video[None],
        grad_text[None],
        grad_mod[None],
        grad_w,
        grad_gain,
    )


def solution(mesh):
    fine = Mesh(mesh.devices.reshape(2, 4, 2, 4, 2), EVERY)
    tokens = P(SECTION, SEQ, None)
    sample = P(SECTION, None, None)
    return jax.shard_map(
        per_device,
        mesh=fine,
        in_specs=(tokens, tokens, P(SECTION), sample, P(), P(), P(None, None, SEQ), P(), tokens, tokens),
        out_specs=(tokens, tokens, tokens, tokens, sample, P(SECTION, None, SEQ), P()),
        check_vma=False,
    )
```

profile of v0, /device:TPU:1, one launch (start us, length us, event | category | flops | bytes accessed | tf_op | source)
XLA Modules:
  0.0 209.3 jit_solution(6448470136268743636)
XLA Ops:
  0.6 1.5 collective-permute-start.3
  2.9 1.1 copy-done.7
  5.5 1.5 collective-permute-start
  7.0 3.8 %collective-permute-start.2 = (bf16[136,3072]{1,0:T(8,128)(2,1)S(1)}, bf16[136,3072]{1,0:T(8,128)(2,1)S(1)}, u32[]{:S(2)}, u32[]{:S(2)}) collective-permute-start(bf16[136,3072]{1,0:T(8,128)(2,1)S(1)} %shard_map.153.refs_0_), channel_id=1, source_target_pairs={{0,6},{2,0},{4,2},{6,4},{1,7},{3,1},{5,3},{7,5},{8,14},{10,8},{12,... | collective-permute-start | bytes 2506760 | tf_op jit(solution)/shard_map/ppermute | solution.py:335
  11.5 0.8 copy-done.16
  12.3 10.2 %shard_map.155 = bf16[16,136,128]{2,1,0:T(8,128)(2,1)} custom-call(bf16[128,3072]{1,0:T(8,128)(2,1)S(1)} %bitcast.40, bf16[8,3072]{1,0:T(8,128)(2,1)S(1)} %bitcast.48, f32[1,3072]{1,0:T(1,128)S(1)} %slice_bitcast_fusion.gate_ref, bf16[2048,3072]{1,0:T(8,128)(2,1)} %w_ref.3), custom_call_target="tpu_custom_call" | custom-call | flops 1 | bytes 1 | tf_op jit(solution)/shard_map/pallas_call | solution.py:368
  22.5 3.2 %collective-permute-done.refs_1_.y_ref = bf16[136,3072]{1,0:T(8,128)(2,1)S(1)} collective-permute-done((bf16[136,3072]{1,0:T(8,128)(2,1)S(1)}, bf16[136,3072]{1,0:T(8,128)(2,1)S(1)}, u32[]{:S(2)}, u32[]{:S(2)}) %collective-permute-start) | collective-permute-done | bytes 835616 | tf_op jit(solution)/shard_map/ppermute | solution.py:335
  25.7 2.6 %collective-permute-done.2.refs_3_.b_ref = bf16[136,3072]{1,0:T(8,128)(2,1)S(1)} collective-permute-done((bf16[136,3072]{1,0:T(8,128)(2,1)S(1)}, bf16[136,3072]{1,0:T(8,128)(2,1)S(1)}, u32[]{:S(2)}, u32[]{:S(2)}) %collective-permute-start.2) | collective-permute-done | bytes 835616 | tf_op jit(solution)/shard_map/ppermute | solution.py:335
  28.3 3.1 %collective-permute-done.1.refs_2_.a_ref = bf16[136,3072]{1,0:T(8,128)(2,1)S(1)} collective-permute-done((bf16[136,3072]{1,0:T(8,128)(2,1)S(1)}, bf16[136,3072]{1,0:T(8,128)(2,1)S(1)}, u32[]{:S(2)}, u32[]{:S(2)}) %collective-permute-start.1) | collective-permute-done | bytes 835616 | tf_op jit(solution)/shard_map/ppermute | solution.py:335
  32.0 1.1 collective-permute-start.6
  33.3 7.6 %shard_map.154 = (bf16[544,3072]{1,0:T(8,128)(2,1)}, bf16[544,384]{1,0:T(8,128)(2,1)}, bf16[544,384]{1,0:T(8,128)(2,1)}) custom-call(bf16[136,3072]{1,0:T(8,128)(2,1)} %copy-done.4, bf16[136,3072]{1,0:T(8,128)(2,1)} %copy-done.1, bf16[136,3072]{1,0:T(8,128)(2,1)} %copy-done.3, bf16[136,3072]{1,0:T(8,128)(2,1)} %copy-done.2, bf16[3,3072,128]{2,1,0:T(8,128)(2,1)} %bitcast.54, ...), custom_call_target="tpu_custom_call" | custom-call | flops 1 | bytes 1 | tf_op jit(solution)/shard_map/pallas_call | solution.py:392
  40.9 1.0 collective-permute-done.8.refs_4_
  41.9 1.7 collective-permute-start.10
  43.7 2.7 %collective-permute-start.5 = (bf16[72,3072]{1,0:T(8,128)(2,1)S(1)}, bf16[72,3072]{1,0:T(8,128)(2,1)}, u32[]{:S(2)}, u32[]{:S(2)}) collective-permute-start(bf16[72,3072]{1,0:T(8,128)(2,1)S(1)} %get-tuple-element.68), channel_id=1, source_target_pairs={{0,6},{2,0},{4,2},{6,4},{1,7},{3,1},{5,3},{7,5},{8,14},{10,8},{12,... | collective-permute-start | bytes 1327112 | tf_op jit(solution)/shard_map/ppermute | solution.py:335
  47.1 6.2 %collective-permute-done.9.refs_5_ = bf16[64,3072]{1,0:T(8,128)(2,1)S(1)} collective-permute-done((bf16[64,3072]{1,0:T(8,128)(2,1)}, bf16[64,3072]{1,0:T(8,128)(2,1)S(1)}, u32[]{:S(2)}, u32[]{:S(2)}) %collective-permute-start.9) | collective-permute-done | bytes 393248 | tf_op jit(solution)/shard_map/ppermute | solution.py:335
  54.1 9.6 %all-to-all-start = ((bf16[16,136,128]{2,1,0:T(8,128)(2,1)}), bf16[16,136,128]{2,1,0:T(8,128)(2,1)S(1)}, u32[]{:S(2)}, u32[]{:S(2)}) async-start(bf16[16,136,128]{2,1,0:T(8,128)(2,1)} %shard_map.155), calls=%async_computation | async-start | bytes 1114112 | tf_op jit(solution)/shard_map/all_to_all | solution.py:410
  63.7 7.8 %shard_map.157 = (bf16[544,3072]{1,0:T(8,128)(2,1)}, bf16[544,384]{1,0:T(8,128)(2,1)}, bf16[544,384]{1,0:T(8,128)(2,1)}) custom-call(bf16[64,3072]{1,0:T(8,128)(2,1)} %collective-permute-done.4.refs_0_, bf16[72,3072]{1,0:T(8,128)(2,1)} %collective-permute-done.5.refs_1_, bf16[64,3072]{1,0:T(8,128)(2,1)} %collective-permute-done.6.refs_2_, ...), custom_call_target="tpu_custom_call" | custom-call | flops 1 | bytes 1 | tf_op jit(solution)/shard_map/pallas_call | solution.py:392
  71.6 1.5 collective-permute-start.11
  76.2 22.9 %shard_map.158 = (bf16[16,144,128]{2,1,0:T(8,128)(2,1)}, bf16[1088,384]{1,0:T(8,128)(2,1)}, bf16[1088,384]{1,0:T(8,128)(2,1)}) custom-call(s32[16]{0:T(128)} %copy-done.30, bf16[544,384]{1,0:T(8,128)(2,1)} %get-tuple-element.64.q1_ref, bf16[544,384]{1,0:T(8,128)(2,1)} %get-tuple-element.74.q2_ref, bf16[544,384]{1,0:T(8,128)(2,1)} %copy-done.27, ...), custom_call_target="tpu_custom_call" | custom-call | flops 1 | bytes 1 | tf_op jit(solution)/shard_map/pallas_call | solution.py:424
  100.1 4.5 %all-to-all-start.1 = ((bf16[16,144,128]{2,1,0:T(8,128)(2,1)}), bf16[16,144,128]{2,1,0:T(8,128)(2,1)S(1)}, u32[]{:S(2)}, u32[]{:S(2)}) async-start(bf16[16,144,128]{2,1,0:T(8,128)(2,1)} %get-tuple-element.79), calls=%async_computation.1 | async-start | bytes 1179648 | tf_op jit(solution)/shard_map/all_to_all | solution.py:452
  104.7 0.9 copy-done.24
  105.6 6.4 %shard_map.159 = (bf16[64,3072]{1,0:T(8,128)(2,1)}, bf16[72,3072]{1,0:T(8,128)(2,1)}, bf16[128,3072]{1,0:T(8,128)(2,1)}, bf16[144,3072]{1,0:T(8,128)(2,1)}, bf16[136,3072]{1,0:T(8,128)(2,1)}) custom-call(bf16[1088,384]{1,0:T(8,128)(2,1)} %get-tuple-element.83.own_ref, bf16[1088,384]{1,0:T(8,128)(2,1)} %copy-done.24, bf16[3,3072,128]{2,1,0:T(8,128)(2,1)} %bitcast.56, ...), custom_call_target="tpu_custom_call" | custom-call | flops 1 | bytes 1 | tf_op jit(solution)/shard_map/pallas_call | solution.py:462
  112.0 1.5 collective-permute-start.19
  113.5 2.4 %collective-permute-start.15 = (bf16[64,3072]{1,0:T(8,128)(2,1)}, bf16[64,3072]{1,0:T(8,128)(2,1)S(1)}, u32[]{:S(2)}, u32[]{:S(2)}) collective-permute-start(bf16[64,3072]{1,0:T(8,128)(2,1)} %get-tuple-element.99), channel_id=1, source_target_pairs={{0,6},{2,0},{4,2},{6,4},{1,7},{3,1},{5,3},{7,5},{8,14},{10,8},{12,... | collective-permute-start | bytes 1179656 | tf_op jit(solution)/shard_map/ppermute | solution.py:335
  115.9 11.8 %shard_map.161 = (bf16[4,2,3,384,128]{4,3,2,1,0:T(8,128)(2,1)}, bf16[4,2,3,384,128]{4,3,2,1,0:T(8,128)(2,1)}) custom-call(s32[2]{0:T(128)} %pad_add_fusion.place_ref, bf16[544,3072]{1,0:T(8,128)(2,1)} %get-tuple-element.86.one_ref, bf16[544,3072]{1,0:T(8,128)(2,1)} %get-tuple-element.87.two_ref, bf16[1088,384]{1,0:T(8,128)(2,1)} %get-tuple-element.83.own_ref, ...), custom_call_target="tpu_custom_call" | custom-call | flops 13200000000 | bytes 1 | tf_op jit(solution)/shard_map/pallas_call | solution.py:471
  127.7 0.9 collective-permute-start.14
  128.6 1.5 shard_map.163
  130.1 3.0 %collective-permute-start.16 = (bf16[128,3072]{1,0:T(8,128)(2,1)}, bf16[128,3072]{1,0:T(8,128)(2,1)}, u32[]{:S(2)}, u32[]{:S(2)}) collective-permute-start(bf16[128,3072]{1,0:T(8,128)(2,1)} %shard_map.163), channel_id=1, source_target_pairs={{0,6},{2,0},{4,2},{6,4},{1,7},{3,1},{5,3},{7,5},{8,14},{10,8},{12,... | collective-permute-start | bytes 2359304 | tf_op jit(solution)/shard_map/ppermute | solution.py:335
  133.1 1.6 shard_map.164
  134.7 6.5 %shard_map.160 = (bf16[136,3072]{1,0:T(8,128)(2,1)}, bf16[136,3072]{1,0:T(8,128)(2,1)}, bf16[136,3072]{1,0:T(8,128)(2,1)}, bf16[136,3072]{1,0:T(8,128)(2,1)}) custom-call(bf16[1088,384]{1,0:T(8,128)(2,1)} %get-tuple-element.83.own_ref, bf16[1088,384]{1,0:T(8,128)(2,1)} %copy-done.24, bf16[3,3072,128]{2,1,0:T(8,128)(2,1)} %bitcast.57, ...), custom_call_target="tpu_custom_call" | custom-call | flops 32999999488 | bytes 1 | tf_op jit(solution)/shard_map/pallas_call | solution.py:488
  141.3 1.4 shard_map.162
  142.7 2.8 %collective-permute-start.21 = (bf16[1160,128]{1,0:T(8,128)(2,1)S(1)}, bf16[1160,128]{1,0:T(8,128)(2,1)S(1)}, u32[]{:S(2)}, u32[]{:S(2)}) collective-permute-start(bf16[1160,128]{1,0:T(8,128)(2,1)S(1)} %get-tuple-element.92), channel_id=1, source_target_pairs={{0,48},{16,0},{32,16},{48,32},{1,49},{17,1},{33,17},{49,33},{2,50}... | collective-permute-start | bytes 890888 | tf_op jit(solution)/shard_map/ppermute | solution.py:335
  145.5 4.8 %collective-permute-done.16.r1_ref = bf16[128,3072]{1,0:T(8,128)(2,1)} collective-permute-done((bf16[128,3072]{1,0:T(8,128)(2,1)}, bf16[128,3072]{1,0:T(8,128)(2,1)}, u32[]{:S(2)}, u32[]{:S(2)}) %collective-permute-start.16) | collective-permute-done | bytes 786464 | tf_op jit(solution)/shard_map/ppermute | solution.py:335
  150.3 6.8 %collective-permute-done.18.r2_ref = bf16[144,3072]{1,0:T(8,128)(2,1)} collective-permute-done((bf16[144,3072]{1,0:T(8,128)(2,1)}, bf16[144,3072]{1,0:T(8,128)(2,1)}, u32[]{:S(2)}, u32[]{:S(2)}) %collective-permute-start.18) | collective-permute-done | bytes 884768 | tf_op jit(solution)/shard_map/ppermute | solution.py:335
  157.2 4.0 %shard_map.165 = (bf16[136,3072]{1,0:T(8,128)(2,1)S(1)}, bf16[136,3072]{1,0:T(8,128)(2,1)}, bf16[136,3072]{1,0:T(8,128)(2,1)}) custom-call(bf16[136,3072]{1,0:T(8,128)(2,1)S(1)} %copy-done.11, bf16[136,3072]{1,0:T(8,128)(2,1)S(1)} %copy-done.12, bf16[136,3072]{1,0:T(8,128)(2,1)S(1)} %copy-done.13, bf16[128,3072]{1,0:T(8,128)(2,1)} %collective-permute-done.16.r1_ref, ...), custom_call_target="tpu_custom_call" | custom-call | flops 1 | bytes 1 | tf_op jit(solution)/shard_map/pallas_call | solution.py:521
  161.2 1.5 collective-permute-start.25
  162.9 2.5 %shard_map.166 = (bf16[2312,128]{1,0:T(8,128)(2,1)}, bf16[2304,128]{1,0:T(8,128)(2,1)}, f32[2,128]{1,0:T(2,128)S(1)}) custom-call(bf16[4,2,3,384,128]{4,3,2,1,0:T(8,128)(2,1)S(1)} %copy-done, bf16[4,2,3,384,128]{4,3,2,1,0:T(8,128)(2,1)} %collective-permute-done.14.got_ref.ag_ref.bg_ref, bf16[4,2,3,384,128]{4,3,2,1,0:T(8,128)(2,1)S(1)} %copy-done, ...), custom_call_target="tpu_custom_call" | custom-call | flops 1 | bytes 1 | tf_op jit(solution)/shard_map/pallas_call | solution.py:532
  165.4 2.5 %collective-permute-start.23 = (bf16[2304,128]{1,0:T(8,128)(2,1)}, bf16[2304,128]{1,0:T(8,128)(2,1)S(1)}, u32[]{:S(2)}, u32[]{:S(2)}) collective-permute-start(bf16[2304,128]{1,0:T(8,128)(2,1)} %get-tuple-element.106), channel_id=1, source_target_pairs={{0,48},{16,0},{32,16},{48,32},{1,49},{17,1},{33,17},{49,33},{2,50}... | collective-permute-start | bytes 1769480 | tf_op jit(solution)/shard_map/ppermute | solution.py:335
  167.8 7.9 %shard_map.167 = (bf16[128,3072]{1,0:T(8,128)(2,1)}, bf16[8,3072]{1,0:T(8,128)(2,1)}, f32[1,3072]{1,0:T(1,128)}) custom-call(bf16[16,144,128]{2,1,0:T(8,128)(2,1)} %copy-done.9, bf16[2048,3072]{1,0:T(8,128)(2,1)} %w_ref.3, bf16[128,3072]{1,0:T(8,128)(2,1)} %bitcast.42, bf16[8,3072]{1,0:T(8,128)(2,1)} %bitcast.50, bf16[128,3072]{1,0:T(8,128)(2,1)} %bitcast.39, ...), custom_call_target="tpu_custom_call" | custom-call | flops 8800000000 | bytes 1 | tf_op jit(solution)/shard_map/pallas_call | solution.py:553
  175.8 3.0 %collective-permute-done.23.b_ref = bf16[2304,128]{1,0:T(8,128)(2,1)S(1)} collective-permute-done((bf16[2304,128]{1,0:T(8,128)(2,1)}, bf16[2304,128]{1,0:T(8,128)(2,1)S(1)}, u32[]{:S(2)}, u32[]{:S(2)}) %collective-permute-start.23) | collective-permute-done | bytes 589856 | tf_op jit(solution)/shard_map/ppermute | solution.py:335
  178.8 3.1 %collective-permute-done.22.a_ref = bf16[2312,128]{1,0:T(8,128)(2,1)S(1)} collective-permute-done((bf16[2312,128]{1,0:T(8,128)(2,1)}, bf16[2312,128]{1,0:T(8,128)(2,1)S(1)}, u32[]{:S(2)}, u32[]{:S(2)}) %collective-permute-start.22) | collective-permute-done | bytes 591904 | tf_op jit(solution)/shard_map/ppermute | solution.py:335
  181.9 1.5 shard_map.168
  183.7 2.9 %shard_map.169 = (bf16[128,3072]{1,0:T(8,128)(2,1)}, bf16[8,3072]{1,0:T(8,128)(2,1)}, bf16[16,3,3072]{2,1,0:T(4,128)(2,1)}) custom-call(bf16[136,3072]{1,0:T(8,128)(2,1)S(1)} %copy-done.14, bf16[136,3072]{1,0:T(8,128)(2,1)S(1)} %collective-permute-done.24.ra_ref, bf16[136,3072]{1,0:T(8,128)(2,1)S(1)} %collective-permute-done.25.rb_ref, ...), custom_call_target="tpu_custom_call" | custom-call | flops 1 | bytes 1 | tf_op jit(solution)/shard_map/pallas_call | solution.py:568
  186.5 6.9 %all-to-all-start.2 = ((bf16[16,3,3072]{2,1,0:T(4,128)(2,1)}), bf16[16,3,3072]{2,1,0:T(4,128)(2,1)S(1)}, u32[]{:S(2)}, u32[]{:S(2)}) async-start(bf16[16,3,3072]{2,1,0:T(4,128)(2,1)} %get-tuple-element.118), calls=%async_computation.2 | async-start | bytes 786432 | tf_op jit(solution)/shard_map/all_to_all | solution.py:573
  193.4 2.6 %collective-permute-start.27 = (bf16[1160,128]{1,0:T(8,128)(2,1)S(1)}, bf16[1160,128]{1,0:T(8,128)(2,1)S(1)}, u32[]{:S(2)}, u32[]{:S(2)}) collective-permute-start(bf16[1160,128]{1,0:T(8,128)(2,1)S(1)} %get-tuple-element.111), channel_id=1, source_target_pairs={{0,64},{64,0},{1,65},{65,1},{2,66},{66,2},{3,67},{67,3},{4,68},{68... | collective-permute-start | bytes 890888 | tf_op jit(solution)/shard_map/ppermute | solution.py:335
  196.0 6.1 %all-to-all-done.2 = bf16[16,3,3072]{2,1,0:T(4,128)(2,1)S(1)} async-done(((bf16[16,3,3072]{2,1,0:T(4,128)(2,1)}), bf16[16,3,3072]{2,1,0:T(4,128)(2,1)S(1)}, u32[]{:S(2)}, u32[]{:S(2)}) %all-to-all-start.2) | async-done | bytes 294944 | tf_op jit(solution)/shard_map/all_to_all | solution.py:573
  202.9 5.0 %collective-permute-done.27 = bf16[1160,128]{1,0:T(8,128)(2,1)S(1)} collective-permute-done((bf16[1160,128]{1,0:T(8,128)(2,1)S(1)}, bf16[1160,128]{1,0:T(8,128)(2,1)S(1)}, u32[]{:S(2)}, u32[]{:S(2)}) %collective-permute-start.27) | collective-permute-done | bytes 296992 | tf_op jit(solution)/shard_map/ppermute | solution.py:335
  208.4 0.9 convert_add_fusion
  (106 shorter events, 10.6 us)
Async XLA Ops:
  0.6 10.8 %copy-start.5 = (bf16[1,128,3072]{2,1,0:T(8,128)(2,1)S(1)}, bf16[1,128,3072]{2,1,0:T(8,128)(2,1)}, u32[]{:S(2)}) copy-start(bf16[1,128,3072]{2,1,0:T(8,128)(2,1)} %param.18) | copy-start | bytes 2359300
  0.6 10.8 %collective-permute-start.3 = (bf16[3,3072,128]{2,1,0:T(8,128)(2,1)}, bf16[3,3072,128]{2,1,0:T(8,128)(2,1)S(1)}, u32[]{:S(2)}, u32[]{:S(2)}) collective-permute-start(bf16[3,3072,128]{2,1,0:T(8,128)(2,1)} %bitcast.53), channel_id=1, source_target_pairs={{0,1},{1,0},{2,3},{3,2},{4,5},{5,4},{6,7},{7,6},{8,9},{9,8},{10,11... | collective-permute-start | bytes 7077896 | tf_op jit(solution)/shard_map/ppermute | solution.py:335
  5.5 17.0 %copy-start.4 = (bf16[136,3072]{1,0:T(8,128)(2,1)}, bf16[136,3072]{1,0:T(8,128)(2,1)S(1)}, u32[]{:S(2)}) copy-start(bf16[136,3072]{1,0:T(8,128)(2,1)S(1)} %shard_map.153.refs_0_) | copy-start | bytes 2506756
  5.5 20.2 %collective-permute-start = (bf16[136,3072]{1,0:T(8,128)(2,1)S(1)}, bf16[136,3072]{1,0:T(8,128)(2,1)S(1)}, u32[]{:S(2)}, u32[]{:S(2)}) collective-permute-start(bf16[136,3072]{1,0:T(8,128)(2,1)S(1)} %shard_map.153.refs_0_), channel_id=1, source_target_pairs={{0,8},{8,0},{1,9},{9,1},{2,10},{10,2},{3,11},{11,3},{4,12},{12,4},... | collective-permute-start | bytes 2506760 | tf_op jit(solution)/shard_map/ppermute | solution.py:335
  7.0 21.4 %collective-permute-start.2 = (bf16[136,3072]{1,0:T(8,128)(2,1)S(1)}, bf16[136,3072]{1,0:T(8,128)(2,1)S(1)}, u32[]{:S(2)}, u32[]{:S(2)}) collective-permute-start(bf16[136,3072]{1,0:T(8,128)(2,1)S(1)} %shard_map.153.refs_0_), channel_id=1, source_target_pairs={{0,6},{2,0},{4,2},{6,4},{1,7},{3,1},{5,3},{7,5},{8,14},{10,8},{12,... | collective-permute-start | bytes 2506760 | tf_op jit(solution)/shard_map/ppermute | solution.py:335
  10.7 20.7 %collective-permute-start.1 = (bf16[136,3072]{1,0:T(8,128)(2,1)S(1)}, bf16[136,3072]{1,0:T(8,128)(2,1)S(1)}, u32[]{:S(2)}, u32[]{:S(2)}) collective-permute-start(bf16[136,3072]{1,0:T(8,128)(2,1)S(1)} %shard_map.153.refs_0_), channel_id=1, source_target_pairs={{0,2},{2,4},{4,6},{6,0},{1,3},{3,5},{5,7},{7,1},{8,10},{10,12},{12... | collective-permute-start | bytes 2506760 | tf_op jit(solution)/shard_map/ppermute | solution.py:335
  11.4 11.1 %copy-start.20 = (f32[1,3072]{1,0:T(1,128)}, f32[1,3072]{1,0:T(1,128)S(1)}, u32[]{:S(2)}) copy-start(f32[1,3072]{1,0:T(1,128)S(1)} %slice_bitcast_fusion.gate_ref) | copy-start | bytes 36868
  11.4 11.1 %copy-start.22 = (bf16[3,3072,128]{2,1,0:T(8,128)(2,1)}, bf16[3,3072,128]{2,1,0:T(8,128)(2,1)S(1)}, u32[]{:S(2)}) copy-start(bf16[3,3072,128]{2,1,0:T(8,128)(2,1)S(1)} %collective-permute-done.3.refs_5_.refs_8_.ws_ref) | copy-start | bytes 7077892
  25.7 7.6 %copy-start.1 = (bf16[136,3072]{1,0:T(8,128)(2,1)}, bf16[136,3072]{1,0:T(8,128)(2,1)S(1)}, u32[]{:S(2)}) copy-start(bf16[136,3072]{1,0:T(8,128)(2,1)S(1)} %collective-permute-done.refs_1_.y_ref) | copy-start | bytes 2506756
  28.3 5.0 %copy-start.2 = (bf16[136,3072]{1,0:T(8,128)(2,1)}, bf16[136,3072]{1,0:T(8,128)(2,1)S(1)}, u32[]{:S(2)}) copy-start(bf16[136,3072]{1,0:T(8,128)(2,1)S(1)} %collective-permute-done.2.refs_3_.b_ref) | copy-start | bytes 2506756
  31.4 1.9 copy-start.3
  31.6 10.3 %collective-permute-start.8 = (bf16[72,3072]{1,0:T(8,128)(2,1)S(1)}, bf16[72,3072]{1,0:T(8,128)(2,1)S(1)}, u32[]{:S(2)}, u32[]{:S(2)}) collective-permute-start(bf16[72,3072]{1,0:T(8,128)(2,1)S(1)} %get-tuple-element.71), channel_id=1, source_target_pairs={{0,6},{2,0},{4,2},{6,4},{1,7},{3,1},{5,3},{7,5},{8,14},{10,8},{12,... | collective-permute-start | bytes 1327112 | tf_op jit(solution)/shard_map/ppermute | solution.py:335
  32.0 11.7 %collective-permute-start.6 = (bf16[64,3072]{1,0:T(8,128)(2,1)S(1)}, bf16[64,3072]{1,0:T(8,128)(2,1)}, u32[]{:S(2)}, u32[]{:S(2)}) collective-permute-start(bf16[64,3072]{1,0:T(8,128)(2,1)S(1)} %get-tuple-element.69), channel_id=1, source_target_pairs={{0,2},{2,4},{4,6},{6,0},{1,3},{3,5},{5,7},{7,1},{8,10},{10,12},{12... | collective-permute-start | bytes 1179656 | tf_op jit(solution)/shard_map/ppermute | solution.py:335
  33.1 30.6 %collective-permute-start.7 = (bf16[136,3072]{1,0:T(8,128)(2,1)S(1)}, bf16[136,3072]{1,0:T(8,128)(2,1)}, u32[]{:S(2)}, u32[]{:S(2)}) collective-permute-start(bf16[136,3072]{1,0:T(8,128)(2,1)S(1)} %get-tuple-element.70), channel_id=1, source_target_pairs={{0,8},{8,0},{1,9},{9,1},{2,10},{10,2},{3,11},{11,3},{4,12},{12,4},... | collective-permute-start | bytes 2506760 | tf_op jit(solution)/shard_map/ppermute | solution.py:335
  41.9 21.8 %copy-start.25 = (bf16[72,3072]{1,0:T(8,128)(2,1)}, bf16[72,3072]{1,0:T(8,128)(2,1)S(1)}, u32[]{:S(2)}) copy-start(bf16[72,3072]{1,0:T(8,128)(2,1)S(1)} %collective-permute-done.8.refs_4_) | copy-start | bytes 1327108
  41.9 11.4 %collective-permute-start.10 = (bf16[72,3072]{1,0:T(8,128)(2,1)S(1)}, bf16[72,3072]{1,0:T(8,128)(2,1)S(1)}, u32[]{:S(2)}, u32[]{:S(2)}) collective-permute-start(bf16[72,3072]{1,0:T(8,128)(2,1)S(1)} %collective-permute-done.8.refs_4_), channel_id=1, source_target_pairs={{0,6},{2,0},{4,2},{6,4},{1,7},{3,1},{5,3},{7,5},{8,14},{10,8},{12,... | collective-permute-start | bytes 1327112 | tf_op jit(solution)/shard_map/ppermute | solution.py:335
  43.7 9.6 %collective-permute-start.9 = (bf16[64,3072]{1,0:T(8,128)(2,1)}, bf16[64,3072]{1,0:T(8,128)(2,1)S(1)}, u32[]{:S(2)}, u32[]{:S(2)}) collective-permute-start(bf16[64,3072]{1,0:T(8,128)(2,1)} %collective-permute-done.6.refs_2_), channel_id=1, source_target_pairs={{0,2},{2,4},{4,6},{6,0},{1,3},{3,5},{5,7},{7,1},{8,10},{10,12},{12... | collective-permute-start | bytes 1179656 | tf_op jit(solution)/shard_map/ppermute | solution.py:335
  43.7 20.0 %collective-permute-start.5 = (bf16[72,3072]{1,0:T(8,128)(2,1)S(1)}, bf16[72,3072]{1,0:T(8,128)(2,1)}, u32[]{:S(2)}, u32[]{:S(2)}) collective-permute-start(bf16[72,3072]{1,0:T(8,128)(2,1)S(1)} %get-tuple-element.68), channel_id=1, source_target_pairs={{0,6},{2,0},{4,2},{6,4},{1,7},{3,1},{5,3},{7,5},{8,14},{10,8},{12,... | collective-permute-start | bytes 1327112 | tf_op jit(solution)/shard_map/ppermute | solution.py:335
  46.4 17.3 %collective-permute-start.4 = (bf16[64,3072]{1,0:T(8,128)(2,1)S(1)}, bf16[64,3072]{1,0:T(8,128)(2,1)}, u32[]{:S(2)}, u32[]{:S(2)}) collective-permute-start(bf16[64,3072]{1,0:T(8,128)(2,1)S(1)} %get-tuple-element.67), channel_id=1, source_target_pairs={{0,2},{2,4},{4,6},{6,0},{1,3},{3,5},{5,7},{7,1},{8,10},{10,12},{12... | collective-permute-start | bytes 1179656 | tf_op jit(solution)/shard_map/ppermute | solution.py:335
  47.1 28.2 %copy-start.30 = (s32[16]{0:T(128)}, s32[16]{0:T(128)S(1)}, u32[]{:S(2)}) copy-start(s32[16]{0:T(128)S(1)} %stack.76.order_ref) | copy-start | bytes 196
  53.3 10.4 %copy-start.26 = (bf16[72,3072]{1,0:T(8,128)(2,1)}, bf16[72,3072]{1,0:T(8,128)(2,1)S(1)}, u32[]{:S(2)}) copy-start(bf16[72,3072]{1,0:T(8,128)(2,1)S(1)} %collective-permute-done.10.refs_6_) | copy-start | bytes 1327108
  54.1 21.2 %all-to-all-start = ((bf16[16,136,128]{2,1,0:T(8,128)(2,1)}), bf16[16,136,128]{2,1,0:T(8,128)(2,1)S(1)}, u32[]{:S(2)}, u32[]{:S(2)}) async-start(bf16[16,136,128]{2,1,0:T(8,128)(2,1)} %shard_map.155), calls=%async_computation | async-start | bytes 1114112 | tf_op jit(solution)/shard_map/all_to_all | solution.py:410
  71.6 3.1 %collective-permute-start.11 = (bf16[544,384]{1,0:T(8,128)(2,1)}, bf16[544,384]{1,0:T(8,128)(2,1)S(1)}, u32[]{:S(2)}, u32[]{:S(2)}) collective-permute-start(bf16[544,384]{1,0:T(8,128)(2,1)} %get-tuple-element.76), channel_id=1, source_target_pairs={{0,1},{1,0},{2,3},{3,2},{4,5},{5,4},{6,7},{7,6},{8,9},{9,8},{10,11... | collective-permute-start | bytes 1253384 | tf_op jit(solution)/shard_map/ppermute | solution.py:335
  73.1 2.2 %collective-permute-start.12 = (bf16[544,384]{1,0:T(8,128)(2,1)}, bf16[544,384]{1,0:T(8,128)(2,1)S(1)}, u32[]{:S(2)}, u32[]{:S(2)}) collective-permute-start(bf16[544,384]{1,0:T(8,128)(2,1)} %get-tuple-element.77), channel_id=1, source_target_pairs={{0,1},{1,0},{2,3},{3,2},{4,5},{5,4},{6,7},{7,6},{8,9},{9,8},{10,11... | collective-permute-start | bytes 1253384 | tf_op jit(solution)/shard_map/ppermute | solution.py:335
  99.2 5.5 %collective-permute-start.13 = (bf16[1088,384]{1,0:T(8,128)(2,1)}, bf16[1088,384]{1,0:T(8,128)(2,1)S(1)}, u32[]{:S(2)}, u32[]{:S(2)}) collective-permute-start(bf16[1088,384]{1,0:T(8,128)(2,1)} %get-tuple-element.81), channel_id=1, source_target_pairs={{0,1},{1,0},{2,3},{3,2},{4,5},{5,4},{6,7},{7,6},{8,9},{9,8},{10,11... | collective-permute-start | bytes 2506760 | tf_op jit(solution)/shard_map/ppermute | solution.py:335
  100.1 41.0 %all-to-all-start.1 = ((bf16[16,144,128]{2,1,0:T(8,128)(2,1)}), bf16[16,144,128]{2,1,0:T(8,128)(2,1)S(1)}, u32[]{:S(2)}, u32[]{:S(2)}) async-start(bf16[16,144,128]{2,1,0:T(8,128)(2,1)} %get-tuple-element.79), calls=%async_computation.1 | async-start | bytes 1179648 | tf_op jit(solution)/shard_map/all_to_all | solution.py:452
  112.0 33.5 %collective-permute-start.19 = (bf16[136,3072]{1,0:T(8,128)(2,1)}, bf16[136,3072]{1,0:T(8,128)(2,1)}, u32[]{:S(2)}, u32[]{:S(2)}) collective-permute-start(bf16[136,3072]{1,0:T(8,128)(2,1)} %get-tuple-element.82), channel_id=1, source_target_pairs={{0,8},{8,0},{1,9},{9,1},{2,10},{10,2},{3,11},{11,3},{4,12},{12,4},... | collective-permute-start | bytes 2506760 | tf_op jit(solution)/shard_map/ppermute | solution.py:335
  113.5 15.1 %collective-permute-start.15 = (bf16[64,3072]{1,0:T(8,128)(2,1)}, bf16[64,3072]{1,0:T(8,128)(2,1)S(1)}, u32[]{:S(2)}, u32[]{:S(2)}) collective-permute-start(bf16[64,3072]{1,0:T(8,128)(2,1)} %get-tuple-element.99), channel_id=1, source_target_pairs={{0,6},{2,0},{4,2},{6,4},{1,7},{3,1},{5,3},{7,5},{8,14},{10,8},{12,... | collective-permute-start | bytes 1179656 | tf_op jit(solution)/shard_map/ppermute | solution.py:335
  115.9 17.2 %collective-permute-start.17 = (bf16[72,3072]{1,0:T(8,128)(2,1)}, bf16[72,3072]{1,0:T(8,128)(2,1)S(1)}, u32[]{:S(2)}, u32[]{:S(2)}) collective-permute-start(bf16[72,3072]{1,0:T(8,128)(2,1)} %get-tuple-element.102), channel_id=1, source_target_pairs={{0,2},{2,4},{4,6},{6,0},{1,3},{3,5},{5,7},{7,1},{8,10},{10,12},{12... | collective-permute-start | bytes 1327112 | tf_op jit(solution)/shard_map/ppermute | solution.py:335
  115.9 12.7 %copy-start.15 = (bf16[128,3072]{1,0:T(8,128)(2,1)S(1)}, bf16[128,3072]{1,0:T(8,128)(2,1)}, u32[]{:S(2)}) copy-start(bf16[128,3072]{1,0:T(8,128)(2,1)} %get-tuple-element.98.base_ref) | copy-start | bytes 2359300
  127.7 5.4 %copy-start.10 = (bf16[144,3072]{1,0:T(8,128)(2,1)S(1)}, bf16[144,3072]{1,0:T(8,128)(2,1)}, u32[]{:S(2)}) copy-start(bf16[144,3072]{1,0:T(8,128)(2,1)} %get-tuple-element.101.base_ref) | copy-start | bytes 2654212
  127.7 13.6 %collective-permute-start.14 = (bf16[4,2,3,384,128]{4,3,2,1,0:T(8,128)(2,1)}, bf16[4,2,3,384,128]{4,3,2,1,0:T(8,128)(2,1)}, u32[]{:S(2)}, u32[]{:S(2)}) collective-permute-start(bf16[4,2,3,384,128]{4,3,2,1,0:T(8,128)(2,1)} %get-tuple-element.89), channel_id=1, source_target_pairs={{0,1},{1,0},{2,3},{3,2},{4,5},{5,4},{6,7},{7,6},{8,9},{9,8},{10,11... | collective-permute-start | bytes 7077896 | tf_op jit(solution)/shard_map/ppermute | solution.py:335
  130.1 20.2 %collective-permute-start.16 = (bf16[128,3072]{1,0:T(8,128)(2,1)}, bf16[128,3072]{1,0:T(8,128)(2,1)}, u32[]{:S(2)}, u32[]{:S(2)}) collective-permute-start(bf16[128,3072]{1,0:T(8,128)(2,1)} %shard_map.163), channel_id=1, source_target_pairs={{0,6},{2,0},{4,2},{6,4},{1,7},{3,1},{5,3},{7,5},{8,14},{10,8},{12,... | collective-permute-start | bytes 2359304 | tf_op jit(solution)/shard_map/ppermute | solution.py:335
  134.7 6.6 %copy-start = (bf16[4,2,3,384,128]{4,3,2,1,0:T(8,128)(2,1)S(1)}, bf16[4,2,3,384,128]{4,3,2,1,0:T(8,128)(2,1)}, u32[]{:S(2)}) copy-start(bf16[4,2,3,384,128]{4,3,2,1,0:T(8,128)(2,1)} %get-tuple-element.88.own_ref.ao_ref.bo_ref) | copy-start | bytes 7077892
  134.7 22.4 %collective-permute-start.18 = (bf16[144,3072]{1,0:T(8,128)(2,1)}, bf16[144,3072]{1,0:T(8,128)(2,1)}, u32[]{:S(2)}, u32[]{:S(2)}) collective-permute-start(bf16[144,3072]{1,0:T(8,128)(2,1)} %shard_map.164), channel_id=1, source_target_pairs={{0,2},{2,4},{4,6},{6,0},{1,3},{3,5},{5,7},{7,1},{8,10},{10,12},{12... | collective-permute-start | bytes 2654216 | tf_op jit(solution)/shard_map/ppermute | solution.py:335
  141.2 15.9 %copy-start.11 = (bf16[136,3072]{1,0:T(8,128)(2,1)S(1)}, bf16[136,3072]{1,0:T(8,128)(2,1)}, u32[]{:S(2)}) copy-start(bf16[136,3072]{1,0:T(8,128)(2,1)} %get-tuple-element.94.y_ref) | copy-start | bytes 2506756
  141.2 15.9 %copy-start.12 = (bf16[136,3072]{1,0:T(8,128)(2,1)S(1)}, bf16[136,3072]{1,0:T(8,128)(2,1)}, u32[]{:S(2)}) copy-start(bf16[136,3072]{1,0:T(8,128)(2,1)} %get-tuple-element.95.a_ref) | copy-start | bytes 2506756
  141.2 15.9 %copy-start.13 = (bf16[136,3072]{1,0:T(8,128)(2,1)S(1)}, bf16[136,3072]{1,0:T(8,128)(2,1)}, u32[]{:S(2)}) copy-start(bf16[136,3072]{1,0:T(8,128)(2,1)} %get-tuple-element.96.b_ref) | copy-start | bytes 2506756
  142.7 20.2 %collective-permute-start.21 = (bf16[1160,128]{1,0:T(8,128)(2,1)S(1)}, bf16[1160,128]{1,0:T(8,128)(2,1)S(1)}, u32[]{:S(2)}, u32[]{:S(2)}) collective-permute-start(bf16[1160,128]{1,0:T(8,128)(2,1)S(1)} %get-tuple-element.92), channel_id=1, source_target_pairs={{0,48},{16,0},{32,16},{48,32},{1,49},{17,1},{33,17},{49,33},{2,50}... | collective-permute-start | bytes 890888 | tf_op jit(solution)/shard_map/ppermute | solution.py:335
  145.5 17.4 %collective-permute-start.20 = (bf16[1160,128]{1,0:T(8,128)(2,1)S(1)}, bf16[1160,128]{1,0:T(8,128)(2,1)S(1)}, u32[]{:S(2)}, u32[]{:S(2)}) collective-permute-start(bf16[1160,128]{1,0:T(8,128)(2,1)S(1)} %get-tuple-element.93), channel_id=1, source_target_pairs={{0,16},{16,32},{32,48},{48,0},{1,17},{17,33},{33,49},{49,1},{2,18}... | collective-permute-start | bytes 890888 | tf_op jit(solution)/shard_map/ppermute | solution.py:335
  161.2 22.3 %collective-permute-start.24 = (bf16[136,3072]{1,0:T(8,128)(2,1)}, bf16[136,3072]{1,0:T(8,128)(2,1)S(1)}, u32[]{:S(2)}, u32[]{:S(2)}) collective-permute-start(bf16[136,3072]{1,0:T(8,128)(2,1)} %get-tuple-element.113), channel_id=1, source_target_pairs={{0,6},{2,0},{4,2},{6,4},{1,7},{3,1},{5,3},{7,5},{8,14},{10,8},{12,... | collective-permute-start | bytes 2506760 | tf_op jit(solution)/shard_map/ppermute | solution.py:335
  161.2 22.3 %collective-permute-start.25 = (bf16[136,3072]{1,0:T(8,128)(2,1)}, bf16[136,3072]{1,0:T(8,128)(2,1)S(1)}, u32[]{:S(2)}, u32[]{:S(2)}) collective-permute-start(bf16[136,3072]{1,0:T(8,128)(2,1)} %get-tuple-element.114), channel_id=1, source_target_pairs={{0,2},{2,4},{4,6},{6,0},{1,3},{3,5},{5,7},{7,1},{8,10},{10,12},{12... | collective-permute-start | bytes 2506760 | tf_op jit(solution)/shard_map/ppermute | solution.py:335
  162.6 20.8 %collective-permute-start.26 = (bf16[136,3072]{1,0:T(8,128)(2,1)S(1)}, bf16[136,3072]{1,0:T(8,128)(2,1)S(1)}, u32[]{:S(2)}, u32[]{:S(2)}) collective-permute-start(bf16[136,3072]{1,0:T(8,128)(2,1)S(1)} %get-tuple-element.103), channel_id=1, source_target_pairs={{0,8},{8,0},{1,9},{9,1},{2,10},{10,2},{3,11},{11,3},{4,12},{12,4},... | collective-permute-start | bytes 2506760 | tf_op jit(solution)/shard_map/ppermute | solution.py:335
  165.4 13.4 %collective-permute-start.23 = (bf16[2304,128]{1,0:T(8,128)(2,1)}, bf16[2304,128]{1,0:T(8,128)(2,1)S(1)}, u32[]{:S(2)}, u32[]{:S(2)}) collective-permute-start(bf16[2304,128]{1,0:T(8,128)(2,1)} %get-tuple-element.106), channel_id=1, source_target_pairs={{0,48},{16,0},{32,16},{48,32},{1,49},{17,1},{33,17},{49,33},{2,50}... | collective-permute-start | bytes 1769480 | tf_op jit(solution)/shard_map/ppermute | solution.py:335
  167.8 14.0 %collective-permute-start.22 = (bf16[2312,128]{1,0:T(8,128)(2,1)}, bf16[2312,128]{1,0:T(8,128)(2,1)S(1)}, u32[]{:S(2)}, u32[]{:S(2)}) collective-permute-start(bf16[2312,128]{1,0:T(8,128)(2,1)} %get-tuple-element.105), channel_id=1, source_target_pairs={{0,16},{16,32},{32,48},{48,0},{1,17},{17,33},{33,49},{49,1},{2,18}... | collective-permute-start | bytes 1775624 | tf_op jit(solution)/shard_map/ppermute | solution.py:335
  181.9 1.8 copy-start.17
  186.5 15.6 %all-to-all-start.2 = ((bf16[16,3,3072]{2,1,0:T(4,128)(2,1)}), bf16[16,3,3072]{2,1,0:T(4,128)(2,1)S(1)}, u32[]{:S(2)}, u32[]{:S(2)}) async-start(bf16[16,3,3072]{2,1,0:T(4,128)(2,1)} %get-tuple-element.118), calls=%async_computation.2 | async-start | bytes 786432 | tf_op jit(solution)/shard_map/all_to_all | solution.py:573
  193.4 14.5 %collective-permute-start.27 = (bf16[1160,128]{1,0:T(8,128)(2,1)S(1)}, bf16[1160,128]{1,0:T(8,128)(2,1)S(1)}, u32[]{:S(2)}, u32[]{:S(2)}) collective-permute-start(bf16[1160,128]{1,0:T(8,128)(2,1)S(1)} %get-tuple-element.111), channel_id=1, source_target_pairs={{0,64},{64,0},{1,65},{65,1},{2,66},{66,2},{3,67},{67,3},{4,68},{68... | collective-permute-start | bytes 890888 | tf_op jit(solution)/shard_map/ppermute | solution.py:335
  (14 other events, 17.0 us)
where the time goes:
time: 211 us; the launch traced here: 209 us
  Pallas kernels  97.5 us (46%)
  starting transfers between devices  53.3 us (25%)
  waiting for transfers between devices  46.1 us (22%)
  local copies, waits for them, and re-layouts  8.55 us (4%)
  other arithmetic  2.28 us (1%)
    ppermute x28, waiting for transfers between devices, ring(): lax.ppermute(values, axis, [(i, (i + distance) % size) for i in range(siz...  40 us
    ppermute x28, starting transfers between devices, ring(): lax.ppermute(values, axis, [(i, (i + distance) % size) for i in range(siz...  32.4 us
    pallas_call x1, Pallas kernels, per_device(): call(functools.partial(attn_kernel, rows), (shape((heads, rows + 8, HD)),...  22.9 us
    pallas_call x2, Pallas kernels, project(): call(functools.partial(qkv_kernel, len(parts)), (shape((block, width)), s...  15.4 us
    pallas_call x1, Pallas kernels, per_device(): call(grad_w_kernel, (shape((4, 2, 3, wide, HD)),) * 2, us=12, mib=56, gri...  11.8 us
    pallas_call x1, Pallas kernels, per_device(): call(d_attn_kernel, shape((heads, rows, HD)), grid=(2 * per,), in_specs=[...  10.2 us
    all_to_all x1, starting transfers between devices, per_device(): lax.all_to_all(tie(d_attn, yc_t, yc_l), SEQ, split_axis=0, concat_axis=0,...  9.58 us
    pallas_call x1, Pallas kernels, per_device(): call(out_kernel, (shape((vrows, width)), shape((trows, width)), shape((1,...  7.94 us
  transfers between devices with their start and end apart: 31, of which 13 were waited for; matrix products, arithmetic and copies ran while one was open for 2% of the time, Pallas kernels for 34%

commit v1 on v0

--- a/solution.py
+++ b/solution.py
@@ -134,10 +134,11 @@
     m_ref[...] = jnp.concatenate([ya[cut:], yb[:cut]], axis=0).astype(BF)
 
 
-def add_kernel(base_ref, got_ref, out_ref):
-    n = got_ref.shape[0]
-    out_ref[:n, :] = (base_ref[:n, :].astype(F) + got_ref[...].astype(F)).astype(BF)
-    out_ref[n:, :] = base_ref[n:, :]
+def add_kernel(one_ref, two_ref, got1_ref, got2_ref, out1_ref, out2_ref):
+    for base_ref, got_ref, out_ref in ((one_ref, got1_ref, out1_ref), (two_ref, got2_ref, out2_ref)):
+        n = got_ref.shape[0]
+        out_ref[:n, :] = (base_ref[:n, :].astype(F) + got_ref[...].astype(F)).astype(BF)
+        out_ref[n:, :] = base_ref[n:, :]
 
 
 def sums_kernel(cut, y_ref, a_ref, b_ref, r1_ref, r2_ref, r3_ref, oy_ref, oa_ref, ob_ref):
@@ -268,9 +269,10 @@
     rows, order_ref, q1_ref, q2_ref, s1_ref, s2_ref, bias_ref, do_ref, gq_ref, gk_ref,
     attn_ref, own_ref, give_ref, q_s, kn_s, v_s, dq_s, dk_s, dv_s, gain_s,
 ):
-    block = q1_ref.shape[0]
+    part = q1_ref.shape[0]
+    block = 2 * part
     parts = (q1_ref, q2_ref, s1_ref, s2_ref)
-    outs = ((own_ref, 0), (own_ref, block), (give_ref, 0), (give_ref, block))
+    outs = ((own_ref, 0), (own_ref, part), (give_ref, 0), (give_ref, part))
     per = block // rows
     scale = HD**-0.5
     step = pl.program_id(0)
@@ -279,7 +281,7 @@
     @pl.when(step == 0)
     def _():
         for i, ref in enumerate(parts):
-            at = slice(i * block, (i + 1) * block)
+            at = slice(i * part, (i + 1) * part)
             q_s[at, :] = ref[:, 0:HD]
             xh, _ = rms(ref[:, HD : 2 * HD].astype(F))
             kn_s[at, :] = (xh * gk).astype(BF)
@@ -312,16 +314,16 @@
     gain_s[0:1, :] += jnp.sum(dq * xh, axis=0, keepdims=True) * scale
     dq_s[here, :] = rms_back(dq * (gq * scale), xh, r).astype(BF)
 
-    @pl.when(step == 3)
+    @pl.when(step == 1)
     def _():
         for i, ref in enumerate(parts):
             out, at = outs[i]
-            out[at : at + block, 0:HD] = dq_s[i * block : (i + 1) * block, :]
+            out[at : at + part, 0:HD] = dq_s[i * part : (i + 1) * part, :]
             xh, r = rms(ref[:, HD : 2 * HD].astype(F))
-            dk = dk_s[i * block : (i + 1) * block, :]
+            dk = dk_s[i * part : (i + 1) * part, :]
             gain_s[1:2, :] += jnp.sum(dk * xh, axis=0, keepdims=True)
-            out[at : at + block, HD : 2 * HD] = rms_back(dk * gk, xh, r).astype(BF)
-            out[at : at + block, 2 * HD :] = dv_s[i * block : (i + 1) * block, :].astype(BF)
+            out[at : at + part, HD : 2 * HD] = rms_back(dk * gk, xh, r).astype(BF)
+            out[at : at + part, 2 * HD :] = dv_s[i * part : (i + 1) * part, :].astype(BF)
         gains = gain_s[...]
         high = gains.astype(BF).astype(F)
         low = (gains - high).astype(BF).astype(F)
@@ -427,7 +429,7 @@
         mib=56,
         grid_spec=pltpu.PrefetchScalarGridSpec(
             num_scalar_prefetch=1,
-            grid=(4,),
+            grid=(2,),
             in_specs=[whole(a) for a in ((block, cols),) * 4]
             + [whole((1, 2 * n)), whole((heads, rows, HD)), whole((1, HD)), whole((1, HD))],
             out_specs=[whole((heads, rows + 8, HD)), whole((n, cols)), whole((n, cols))],
@@ -471,7 +473,7 @@
     g_own, g_sib = call(
         grad_w_kernel,
         (shape((4, 2, 3, wide, HD)),) * 2,
-        us=12,
+        us=20,
         mib=56,
         grid_spec=pltpu.PrefetchScalarGridSpec(
             num_scalar_prefetch=1,
@@ -496,16 +498,15 @@
 
     thirds = lambda count: pl.BlockSpec((count, width // 3), lambda i: (0, i))
 
-    def add(base, got):
-        return call(
-            add_kernel,
-            shape(base.shape),
-            grid=(3,),
-            in_specs=[thirds(base.shape[0]), thirds(got.shape[0])],
-            out_specs=thirds(base.shape[0]),
-        )(base, got)
-
-    r_1, r_2 = zm(add(tie(m_1, g_own), r_ya)), zp(add(tie(m_2, g_own), r_yb))
+    m_1, m_2 = call(
+        add_kernel,
+        (shape((2 * cut, width)), shape((2 * part, width))),
+        us=30,
+        grid=(3,),
+        in_specs=[thirds(k) for k in (2 * cut, 2 * part, cut, part)],
+        out_specs=[thirds(2 * cut), thirds(2 * part)],
+    )(tie(m_1, g_own), m_2, r_ya, r_yb)
+    r_1, r_2 = zm(m_1), zp(m_2)
     g_got = cc(g_sib)
     flat = 3 * wide
     pick = lambda r: [pl.BlockSpec((1, 2, 3, wide, HD), lambda i: (r, 0, 0, 0, 0))] * 2
@@ -516,8 +517,15 @@
         grid=(1,),
         in_specs=pick(2) + [pl.BlockSpec((heads, 8, HD), lambda i: (0, rows // 8, 0))],
         out_specs=[whole((flat + 8, HD)), whole((flat + 8, HD)), whole((2, HD))],
-    )(g_own, g_got, tie(attn_tok, p_o))
+    )(g_own, g_got, tie(attn_tok, m_1, m_2))
     got_b, got_a = ring(far_0, "x", -1), ring(far_1, "x", 1)
+    send_a, send_b, gains = call(
+        near_section_kernel,
+        (shape((2 * flat + 8, HD)), shape((2 * flat, HD)), two),
+        grid=(1,),
+        in_specs=pick(1) + pick(3) + [whole((flat + 8, HD))] * 2 + [whole((2, HD))],
+        out_specs=[whole((2 * flat + 8, HD)), whole((2 * flat, HD)), whole((2, HD))],
+    )(g_own, g_got, g_own, g_got, got_a, got_b, tie(gains, p_o))
     p_y, p_a, p_b = call(
         functools.partial(sums_kernel, cut),
         (shape((rows, width)),) * 3,
@@ -525,17 +533,10 @@
         in_specs=[thirds(k) for k in (rows, rows, rows, 2 * cut, 2 * part, rows)],
         out_specs=[thirds(rows)] * 3,
     )(
-        tie(p_y, far_0, far_1), p_a, p_b, r_1, r_2, r_3
+        tie(p_y, send_a, send_b), p_a, p_b, r_1, r_2, r_3
     )
     last_a, last_b, last_y = zm(p_a), zp(p_b), yy(p_y)
 
-    send_a, send_b, gains = call(
-        near_section_kernel,
-        (shape((2 * flat + 8, HD)), shape((2 * flat, HD)), two),
-        grid=(1,),
-        in_specs=pick(1) + pick(3) + [whole((flat + 8, HD))] * 2 + [whole((2, HD))],
-        out_specs=[whole((2 * flat + 8, HD)), whole((2 * flat, HD)), whole((2, HD))],
-    )(g_own, g_got, g_own, g_got, got_a, got_b, gains)
     back_a, back_b = ring(send_a, "x", 1), ring(send_b, "x", -1)
     keep, give, gains = call(
         own_section_kernel,
@@ -563,7 +564,7 @@
         + [strips(k) for k in (vrows, trows, vrows, trows, 1)],
         out_specs=[strips(k) for k in (vrows, trows, 1)],
         scratch_shapes=[pltpu.VMEM((rows, heads * HD), BF)],
-    )(tie(attn_tok, p_y, send_a, send_b), w_out, video, text, cot_video, cot_text, gate)
+    )(tie(attn_tok, p_y), w_out, video, text, cot_video, cot_text, gate)
 
     grad_video, grad_text, wide_mod = call(
         tail_kernel,

time: 211 us -> 202 us (0.957)
  waiting for transfers between devices: 46.1 us -> 37.6 us
  Pallas kernels: 97.5 us -> 94.4 us
    ppermute x28, waiting for transfers between devices: 40 us -> 30.6 us  [ring(): lax.ppermute(values, axis, [(i, (i + distance) % size) for i in range(siz...]
    unnamed x63 -> x67, local copies, waits for them, and re-layouts: 6.39 us -> 7.74 us
    pallas_call x3 -> x2, Pallas kernels: 14.9 us -> 13.7 us  [the longest x1 11.9 us: per_device(): call(grad_w_kernel, (shape((4, 2, 3, wide, HD)),) * 2, us=20, mib=56, gri...]
  transfers between devices with their start and end apart: 31 -> 31, of which waited for: 13 -> 13; matrix products, arithmetic and copies ran while one was open for 2% -> 2% of each run, Pallas kernels for 34% -> 36%
where the time goes in v1:
time: 202 us; the launch traced here: 200 us
  Pallas kernels  94.4 us (47%)
  starting transfers between devices  54.5 us (27%)
  waiting for transfers between devices  37.6 us (19%)
  local copies, waits for them, and re-layouts  9.9 us (5%)
  other arithmetic  2.28 us (1%)
    ppermute x28, starting transfers between devices, ring(): lax.ppermute(values, axis, [(i, (i + distance) % size) for i in range(siz...  32.6 us
    ppermute x28, waiting for transfers between devices, ring(): lax.ppermute(values, axis, [(i, (i + distance) % size) for i in range(siz...  30.6 us
    pallas_call x1, Pallas kernels, per_device(): call(functools.partial(attn_kernel, rows), (shape((heads, rows + 8, HD)),...  22.1 us
    pallas_call x2, Pallas kernels, project(): call(functools.partial(qkv_kernel, len(parts)), (shape((block, width)), s...  15.4 us
    pallas_call x1, Pallas kernels, per_device(): call(grad_w_kernel, (shape((4, 2, 3, wide, HD)),) * 2, us=20, mib=56, gri...  11.9 us
    pallas_call x1, Pallas kernels, per_device(): call(d_attn_kernel, shape((heads, rows, HD)), grid=(2 * per,), in_specs=[...  10.2 us
    all_to_all x1, starting transfers between devices, per_device(): lax.all_to_all(tie(d_attn, yc_t, yc_l), SEQ, split_axis=0, concat_axis=0,...  9.58 us
    pallas_call x1, Pallas kernels, per_device(): call(out_kernel, (shape((vrows, width)), shape((trows, width)), shape((1,...  7.94 us
  transfers between devices with their start and end apart: 31, of which 13 were waited for; matrix products, arithmetic and copies ran while one was open for 2% of the time, Pallas kernels for 36%

profile of v1, /device:TPU:1, one launch (start us, length us, event | category | flops | bytes accessed | tf_op | source)
XLA Modules:
  0.0 200.3 jit_solution(17279337674945909022)
XLA Ops:
  0.6 1.5 collective-permute-start.3
  2.9 1.1 copy-done.7
  5.5 1.5 collective-permute-start
  7.0 3.8 %collective-permute-start.2 = (bf16[136,3072]{1,0:T(8,128)(2,1)S(1)}, bf16[136,3072]{1,0:T(8,128)(2,1)S(1)}, u32[]{:S(2)}, u32[]{:S(2)}) collective-permute-start(bf16[136,3072]{1,0:T(8,128)(2,1)S(1)} %shard_map.153.refs_0_), channel_id=1, source_target_pairs={{0,6},{2,0},{4,2},{6,4},{1,7},{3,1},{5,3},{7,5},{8,14},{10,8},{12,... | collective-permute-start | bytes 2506760 | tf_op jit(solution)/shard_map/ppermute | solution.py:337
  12.3 10.2 %shard_map.155 = bf16[16,136,128]{2,1,0:T(8,128)(2,1)} custom-call(bf16[128,3072]{1,0:T(8,128)(2,1)S(1)} %bitcast.40, bf16[8,3072]{1,0:T(8,128)(2,1)S(1)} %bitcast.48, f32[1,3072]{1,0:T(1,128)S(1)} %slice_bitcast_fusion.gate_ref, bf16[2048,3072]{1,0:T(8,128)(2,1)} %w_ref.3), custom_call_target="tpu_custom_call" | custom-call | flops 1 | bytes 1 | tf_op jit(solution)/shard_map/pallas_call | solution.py:370
  22.5 3.2 %collective-permute-done.refs_1_.y_ref = bf16[136,3072]{1,0:T(8,128)(2,1)S(1)} collective-permute-done((bf16[136,3072]{1,0:T(8,128)(2,1)S(1)}, bf16[136,3072]{1,0:T(8,128)(2,1)S(1)}, u32[]{:S(2)}, u32[]{:S(2)}) %collective-permute-start) | collective-permute-done | bytes 835616 | tf_op jit(solution)/shard_map/ppermute | solution.py:337
  25.7 2.6 %collective-permute-done.2.refs_3_.b_ref = bf16[136,3072]{1,0:T(8,128)(2,1)S(1)} collective-permute-done((bf16[136,3072]{1,0:T(8,128)(2,1)S(1)}, bf16[136,3072]{1,0:T(8,128)(2,1)S(1)}, u32[]{:S(2)}, u32[]{:S(2)}) %collective-permute-start.2) | collective-permute-done | bytes 835616 | tf_op jit(solution)/shard_map/ppermute | solution.py:337
  28.3 3.1 %collective-permute-done.1.refs_2_.a_ref = bf16[136,3072]{1,0:T(8,128)(2,1)S(1)} collective-permute-done((bf16[136,3072]{1,0:T(8,128)(2,1)S(1)}, bf16[136,3072]{1,0:T(8,128)(2,1)S(1)}, u32[]{:S(2)}, u32[]{:S(2)}) %collective-permute-start.1) | collective-permute-done | bytes 835616 | tf_op jit(solution)/shard_map/ppermute | solution.py:337
  32.0 1.1 collective-permute-start.6
  33.3 7.6 %shard_map.154 = (bf16[544,3072]{1,0:T(8,128)(2,1)}, bf16[544,384]{1,0:T(8,128)(2,1)}, bf16[544,384]{1,0:T(8,128)(2,1)}) custom-call(bf16[136,3072]{1,0:T(8,128)(2,1)} %copy-done.4, bf16[136,3072]{1,0:T(8,128)(2,1)} %copy-done.1, bf16[136,3072]{1,0:T(8,128)(2,1)} %copy-done.3, bf16[136,3072]{1,0:T(8,128)(2,1)} %copy-done.2, bf16[3,3072,128]{2,1,0:T(8,128)(2,1)} %bitcast.54, ...), custom_call_target="tpu_custom_call" | custom-call | flops 1 | bytes 1 | tf_op jit(solution)/shard_map/pallas_call | solution.py:394
  40.9 1.0 collective-permute-done.8.refs_4_
  41.9 1.7 collective-permute-start.10
  43.7 2.7 %collective-permute-start.5 = (bf16[72,3072]{1,0:T(8,128)(2,1)S(1)}, bf16[72,3072]{1,0:T(8,128)(2,1)}, u32[]{:S(2)}, u32[]{:S(2)}) collective-permute-start(bf16[72,3072]{1,0:T(8,128)(2,1)S(1)} %get-tuple-element.70), channel_id=1, source_target_pairs={{0,6},{2,0},{4,2},{6,4},{1,7},{3,1},{5,3},{7,5},{8,14},{10,8},{12,... | collective-permute-start | bytes 1327112 | tf_op jit(solution)/shard_map/ppermute | solution.py:337
  47.1 6.2 %collective-permute-done.9.refs_5_ = bf16[64,3072]{1,0:T(8,128)(2,1)S(1)} collective-permute-done((bf16[64,3072]{1,0:T(8,128)(2,1)}, bf16[64,3072]{1,0:T(8,128)(2,1)S(1)}, u32[]{:S(2)}, u32[]{:S(2)}) %collective-permute-start.9) | collective-permute-done | bytes 393248 | tf_op jit(solution)/shard_map/ppermute | solution.py:337
  54.1 9.6 %all-to-all-start = ((bf16[16,136,128]{2,1,0:T(8,128)(2,1)}), bf16[16,136,128]{2,1,0:T(8,128)(2,1)S(1)}, u32[]{:S(2)}, u32[]{:S(2)}) async-start(bf16[16,136,128]{2,1,0:T(8,128)(2,1)} %shard_map.155), calls=%async_computation | async-start | bytes 1114112 | tf_op jit(solution)/shard_map/all_to_all | solution.py:412
  63.7 7.8 %shard_map.157 = (bf16[544,3072]{1,0:T(8,128)(2,1)}, bf16[544,384]{1,0:T(8,128)(2,1)}, bf16[544,384]{1,0:T(8,128)(2,1)}) custom-call(bf16[64,3072]{1,0:T(8,128)(2,1)} %collective-permute-done.4.refs_0_, bf16[72,3072]{1,0:T(8,128)(2,1)} %collective-permute-done.5.refs_1_, bf16[64,3072]{1,0:T(8,128)(2,1)} %collective-permute-done.6.refs_2_, ...), custom_call_target="tpu_custom_call" | custom-call | flops 1 | bytes 1 | tf_op jit(solution)/shard_map/pallas_call | solution.py:394
  71.5 1.6 collective-permute-start.11
  76.2 22.1 %shard_map.158 = (bf16[16,144,128]{2,1,0:T(8,128)(2,1)}, bf16[1088,384]{1,0:T(8,128)(2,1)}, bf16[1088,384]{1,0:T(8,128)(2,1)}) custom-call(s32[16]{0:T(128)} %copy-done.32, bf16[544,384]{1,0:T(8,128)(2,1)} %get-tuple-element.66.q1_ref, bf16[544,384]{1,0:T(8,128)(2,1)} %get-tuple-element.76.q2_ref, bf16[544,384]{1,0:T(8,128)(2,1)} %copy-done.29, ...), custom_call_target="tpu_custom_call" | custom-call | flops 1 | bytes 1 | tf_op jit(solution)/shard_map/pallas_call | solution.py:426
  99.3 4.5 %all-to-all-start.1 = ((bf16[16,144,128]{2,1,0:T(8,128)(2,1)}), bf16[16,144,128]{2,1,0:T(8,128)(2,1)S(1)}, u32[]{:S(2)}, u32[]{:S(2)}) async-start(bf16[16,144,128]{2,1,0:T(8,128)(2,1)} %get-tuple-element.81), calls=%async_computation.1 | async-start | bytes 1179648 | tf_op jit(solution)/shard_map/all_to_all | solution.py:454
  103.8 0.9 copy-done.26
  104.7 6.4 %shard_map.159 = (bf16[64,3072]{1,0:T(8,128)(2,1)}, bf16[72,3072]{1,0:T(8,128)(2,1)}, bf16[128,3072]{1,0:T(8,128)(2,1)}, bf16[144,3072]{1,0:T(8,128)(2,1)}, bf16[136,3072]{1,0:T(8,128)(2,1)}) custom-call(bf16[1088,384]{1,0:T(8,128)(2,1)} %get-tuple-element.85.own_ref, bf16[1088,384]{1,0:T(8,128)(2,1)} %copy-done.26, bf16[3,3072,128]{2,1,0:T(8,128)(2,1)} %bitcast.56, ...), custom_call_target="tpu_custom_call" | custom-call | flops 1 | bytes 1 | tf_op jit(solution)/shard_map/pallas_call | solution.py:464
  111.1 1.5 collective-permute-start.21
  112.6 2.4 %collective-permute-start.15 = (bf16[64,3072]{1,0:T(8,128)(2,1)}, bf16[64,3072]{1,0:T(8,128)(2,1)S(1)}, u32[]{:S(2)}, u32[]{:S(2)}) collective-permute-start(bf16[64,3072]{1,0:T(8,128)(2,1)} %get-tuple-element.95), channel_id=1, source_target_pairs={{0,6},{2,0},{4,2},{6,4},{1,7},{3,1},{5,3},{7,5},{8,14},{10,8},{12,... | collective-permute-start | bytes 1179656 | tf_op jit(solution)/shard_map/ppermute | solution.py:337
  115.0 11.9 %shard_map.161 = (bf16[4,2,3,384,128]{4,3,2,1,0:T(8,128)(2,1)}, bf16[4,2,3,384,128]{4,3,2,1,0:T(8,128)(2,1)}) custom-call(s32[2]{0:T(128)} %pad_add_fusion.place_ref, bf16[544,3072]{1,0:T(8,128)(2,1)} %get-tuple-element.88.one_ref, bf16[544,3072]{1,0:T(8,128)(2,1)} %get-tuple-element.89.two_ref, bf16[1088,384]{1,0:T(8,128)(2,1)} %get-tuple-element.85.own_ref, ...), custom_call_target="tpu_custom_call" | custom-call | flops 22000001024 | bytes 1 | tf_op jit(solution)/shard_map/pallas_call | solution.py:473
  126.8 0.9 collective-permute-start.14
  127.8 1.9 shard_map.162
  129.6 3.0 %collective-permute-start.19 = (bf16[128,3072]{1,0:T(8,128)(2,1)}, bf16[128,3072]{1,0:T(8,128)(2,1)}, u32[]{:S(2)}, u32[]{:S(2)}) collective-permute-start(bf16[128,3072]{1,0:T(8,128)(2,1)} %get-tuple-element.97), channel_id=1, source_target_pairs={{0,6},{2,0},{4,2},{6,4},{1,7},{3,1},{5,3},{7,5},{8,14},{10,8},{12,... | collective-permute-start | bytes 2359304 | tf_op jit(solution)/shard_map/ppermute | solution.py:337
  132.6 1.4 shard_map.163
  134.0 1.3 collective-permute-start.17
  135.3 1.5 collective-permute-start.18
  136.8 6.4 %shard_map.160 = (bf16[136,3072]{1,0:T(8,128)(2,1)}, bf16[136,3072]{1,0:T(8,128)(2,1)}, bf16[136,3072]{1,0:T(8,128)(2,1)}, bf16[136,3072]{1,0:T(8,128)(2,1)}) custom-call(bf16[1088,384]{1,0:T(8,128)(2,1)} %get-tuple-element.85.own_ref, bf16[1088,384]{1,0:T(8,128)(2,1)} %copy-done.26, bf16[3,3072,128]{2,1,0:T(8,128)(2,1)} %bitcast.57, ...), custom_call_target="tpu_custom_call" | custom-call | flops 32999999488 | bytes 1 | tf_op jit(solution)/shard_map/pallas_call | solution.py:490
  143.8 1.7 shard_map.164
  145.5 0.8 collective-permute-start.22
  146.3 1.9 collective-permute-start.23
  148.3 1.6 collective-permute-done.19.r1_ref
  149.9 5.2 %collective-permute-done.20.r2_ref = bf16[144,3072]{1,0:T(8,128)(2,1)} collective-permute-done((bf16[144,3072]{1,0:T(8,128)(2,1)}, bf16[144,3072]{1,0:T(8,128)(2,1)}, u32[]{:S(2)}, u32[]{:S(2)}) %collective-permute-start.20) | collective-permute-done | bytes 884768 | tf_op jit(solution)/shard_map/ppermute | solution.py:337
  155.1 4.1 %shard_map.165 = (bf16[136,3072]{1,0:T(8,128)(2,1)}, bf16[136,3072]{1,0:T(8,128)(2,1)}, bf16[136,3072]{1,0:T(8,128)(2,1)}) custom-call(bf16[136,3072]{1,0:T(8,128)(2,1)S(1)} %copy-done.10, bf16[136,3072]{1,0:T(8,128)(2,1)S(1)} %copy-done.11, bf16[136,3072]{1,0:T(8,128)(2,1)S(1)} %copy-done.12, bf16[128,3072]{1,0:T(8,128)(2,1)} %collective-permute-done.19.r1_ref, ...), custom_call_target="tpu_custom_call" | custom-call | flops 1 | bytes 1 | tf_op jit(solution)/shard_map/pallas_call | solution.py:529
  159.2 1.5 collective-permute-start.25
  160.9 1.4 shard_map.167
  162.3 0.8 copy-done.14
  163.2 2.6 %collective-permute-start.27 = (bf16[1160,128]{1,0:T(8,128)(2,1)S(1)}, bf16[1160,128]{1,0:T(8,128)(2,1)S(1)}, u32[]{:S(2)}, u32[]{:S(2)}) collective-permute-start(bf16[1160,128]{1,0:T(8,128)(2,1)S(1)} %get-tuple-element.115), channel_id=1, source_target_pairs={{0,64},{64,0},{1,65},{65,1},{2,66},{66,2},{3,67},{67,3},{4,68},{68... | collective-permute-start | bytes 890888 | tf_op jit(solution)/shard_map/ppermute | solution.py:337
  165.8 7.9 %shard_map.166 = (bf16[128,3072]{1,0:T(8,128)(2,1)}, bf16[8,3072]{1,0:T(8,128)(2,1)}, f32[1,3072]{1,0:T(1,128)}) custom-call(bf16[16,144,128]{2,1,0:T(8,128)(2,1)} %copy-done.9, bf16[2048,3072]{1,0:T(8,128)(2,1)} %w_ref.3, bf16[128,3072]{1,0:T(8,128)(2,1)} %bitcast.42, bf16[8,3072]{1,0:T(8,128)(2,1)} %bitcast.50, bf16[128,3072]{1,0:T(8,128)(2,1)} %bitcast.39, ...), custom_call_target="tpu_custom_call" | custom-call | flops 8800000000 | bytes 1 | tf_op jit(solution)/shard_map/pallas_call | solution.py:554
  173.7 4.6 %collective-permute-done.24.ra_ref = bf16[136,3072]{1,0:T(8,128)(2,1)S(1)} collective-permute-done((bf16[136,3072]{1,0:T(8,128)(2,1)}, bf16[136,3072]{1,0:T(8,128)(2,1)S(1)}, u32[]{:S(2)}, u32[]{:S(2)}) %collective-permute-start.24) | collective-permute-done | bytes 835616 | tf_op jit(solution)/shard_map/ppermute | solution.py:337
  178.4 1.2 collective-permute-done.25.rb_ref
  180.3 2.9 %shard_map.168 = (bf16[128,3072]{1,0:T(8,128)(2,1)}, bf16[8,3072]{1,0:T(8,128)(2,1)}, bf16[16,3,3072]{2,1,0:T(4,128)(2,1)}) custom-call(bf16[136,3072]{1,0:T(8,128)(2,1)S(1)} %copy-done.13, bf16[136,3072]{1,0:T(8,128)(2,1)S(1)} %collective-permute-done.24.ra_ref, bf16[136,3072]{1,0:T(8,128)(2,1)S(1)} %collective-permute-done.25.rb_ref, ...), custom_call_target="tpu_custom_call" | custom-call | flops 1 | bytes 1 | tf_op jit(solution)/shard_map/pallas_call | solution.py:569
  183.2 7.8 %all-to-all-start.2 = ((bf16[16,3,3072]{2,1,0:T(4,128)(2,1)}), bf16[16,3,3072]{2,1,0:T(4,128)(2,1)S(1)}, u32[]{:S(2)}, u32[]{:S(2)}) async-start(bf16[16,3,3072]{2,1,0:T(4,128)(2,1)} %get-tuple-element.122), calls=%async_computation.2 | async-start | bytes 786432 | tf_op jit(solution)/shard_map/all_to_all | solution.py:574
  191.0 0.9 convert_add_fusion
  192.5 7.0 %all-to-all-done.2 = bf16[16,3,3072]{2,1,0:T(4,128)(2,1)S(1)} async-done(((bf16[16,3,3072]{2,1,0:T(4,128)(2,1)}), bf16[16,3,3072]{2,1,0:T(4,128)(2,1)S(1)}, u32[]{:S(2)}, u32[]{:S(2)}) %all-to-all-start.2) | async-done | bytes 294944 | tf_op jit(solution)/shard_map/all_to_all | solution.py:574
  (109 shorter events, 12.5 us)
Async XLA Ops:
  0.6 10.8 %copy-start.5 = (bf16[1,128,3072]{2,1,0:T(8,128)(2,1)S(1)}, bf16[1,128,3072]{2,1,0:T(8,128)(2,1)}, u32[]{:S(2)}) copy-start(bf16[1,128,3072]{2,1,0:T(8,128)(2,1)} %param.18) | copy-start | bytes 2359300
  0.6 10.8 %collective-permute-start.3 = (bf16[3,3072,128]{2,1,0:T(8,128)(2,1)}, bf16[3,3072,128]{2,1,0:T(8,128)(2,1)S(1)}, u32[]{:S(2)}, u32[]{:S(2)}) collective-permute-start(bf16[3,3072,128]{2,1,0:T(8,128)(2,1)} %bitcast.53), channel_id=1, source_target_pairs={{0,1},{1,0},{2,3},{3,2},{4,5},{5,4},{6,7},{7,6},{8,9},{9,8},{10,11... | collective-permute-start | bytes 7077896 | tf_op jit(solution)/shard_map/ppermute | solution.py:337
  5.5 17.0 %copy-start.4 = (bf16[136,3072]{1,0:T(8,128)(2,1)}, bf16[136,3072]{1,0:T(8,128)(2,1)S(1)}, u32[]{:S(2)}) copy-start(bf16[136,3072]{1,0:T(8,128)(2,1)S(1)} %shard_map.153.refs_0_) | copy-start | bytes 2506756
  5.5 20.2 %collective-permute-start = (bf16[136,3072]{1,0:T(8,128)(2,1)S(1)}, bf16[136,3072]{1,0:T(8,128)(2,1)S(1)}, u32[]{:S(2)}, u32[]{:S(2)}) collective-permute-start(bf16[136,3072]{1,0:T(8,128)(2,1)S(1)} %shard_map.153.refs_0_), channel_id=1, source_target_pairs={{0,8},{8,0},{1,9},{9,1},{2,10},{10,2},{3,11},{11,3},{4,12},{12,4},... | collective-permute-start | bytes 2506760 | tf_op jit(solution)/shard_map/ppermute | solution.py:337
  7.0 21.4 %collective-permute-start.2 = (bf16[136,3072]{1,0:T(8,128)(2,1)S(1)}, bf16[136,3072]{1,0:T(8,128)(2,1)S(1)}, u32[]{:S(2)}, u32[]{:S(2)}) collective-permute-start(bf16[136,3072]{1,0:T(8,128)(2,1)S(1)} %shard_map.153.refs_0_), channel_id=1, source_target_pairs={{0,6},{2,0},{4,2},{6,4},{1,7},{3,1},{5,3},{7,5},{8,14},{10,8},{12,... | collective-permute-start | bytes 2506760 | tf_op jit(solution)/shard_map/ppermute | solution.py:337
  10.7 20.7 %collective-permute-start.1 = (bf16[136,3072]{1,0:T(8,128)(2,1)S(1)}, bf16[136,3072]{1,0:T(8,128)(2,1)S(1)}, u32[]{:S(2)}, u32[]{:S(2)}) collective-permute-start(bf16[136,3072]{1,0:T(8,128)(2,1)S(1)} %shard_map.153.refs_0_), channel_id=1, source_target_pairs={{0,2},{2,4},{4,6},{6,0},{1,3},{3,5},{5,7},{7,1},{8,10},{10,12},{12... | collective-permute-start | bytes 2506760 | tf_op jit(solution)/shard_map/ppermute | solution.py:337
  11.4 11.1 %copy-start.20 = (f32[1,3072]{1,0:T(1,128)}, f32[1,3072]{1,0:T(1,128)S(1)}, u32[]{:S(2)}) copy-start(f32[1,3072]{1,0:T(1,128)S(1)} %slice_bitcast_fusion.gate_ref) | copy-start | bytes 36868
  11.4 11.0 %copy-start.24 = (bf16[3,3072,128]{2,1,0:T(8,128)(2,1)}, bf16[3,3072,128]{2,1,0:T(8,128)(2,1)S(1)}, u32[]{:S(2)}) copy-start(bf16[3,3072,128]{2,1,0:T(8,128)(2,1)S(1)} %collective-permute-done.3.refs_5_.refs_8_.ws_ref) | copy-start | bytes 7077892
  31.6 10.3 %collective-permute-start.8 = (bf16[72,3072]{1,0:T(8,128)(2,1)S(1)}, bf16[72,3072]{1,0:T(8,128)(2,1)S(1)}, u32[]{:S(2)}, u32[]{:S(2)}) collective-permute-start(bf16[72,3072]{1,0:T(8,128)(2,1)S(1)} %get-tuple-element.73), channel_id=1, source_target_pairs={{0,6},{2,0},{4,2},{6,4},{1,7},{3,1},{5,3},{7,5},{8,14},{10,8},{12,... | collective-permute-start | bytes 1327112 | tf_op jit(solution)/shard_map/ppermute | solution.py:337
  32.0 11.7 %collective-permute-start.6 = (bf16[64,3072]{1,0:T(8,128)(2,1)S(1)}, bf16[64,3072]{1,0:T(8,128)(2,1)}, u32[]{:S(2)}, u32[]{:S(2)}) collective-permute-start(bf16[64,3072]{1,0:T(8,128)(2,1)S(1)} %get-tuple-element.71), channel_id=1, source_target_pairs={{0,2},{2,4},{4,6},{6,0},{1,3},{3,5},{5,7},{7,1},{8,10},{10,12},{12... | collective-permute-start | bytes 1179656 | tf_op jit(solution)/shard_map/ppermute | solution.py:337
  33.1 30.6 %collective-permute-start.7 = (bf16[136,3072]{1,0:T(8,128)(2,1)S(1)}, bf16[136,3072]{1,0:T(8,128)(2,1)}, u32[]{:S(2)}, u32[]{:S(2)}) collective-permute-start(bf16[136,3072]{1,0:T(8,128)(2,1)S(1)} %get-tuple-element.72), channel_id=1, source_target_pairs={{0,8},{8,0},{1,9},{9,1},{2,10},{10,2},{3,11},{11,3},{4,12},{12,4},... | collective-permute-start | bytes 2506760 | tf_op jit(solution)/shard_map/ppermute | solution.py:337
  41.9 21.8 %copy-start.27 = (bf16[72,3072]{1,0:T(8,128)(2,1)}, bf16[72,3072]{1,0:T(8,128)(2,1)S(1)}, u32[]{:S(2)}) copy-start(bf16[72,3072]{1,0:T(8,128)(2,1)S(1)} %collective-permute-done.8.refs_4_) | copy-start | bytes 1327108
  41.9 11.4 %collective-permute-start.10 = (bf16[72,3072]{1,0:T(8,128)(2,1)S(1)}, bf16[72,3072]{1,0:T(8,128)(2,1)S(1)}, u32[]{:S(2)}, u32[]{:S(2)}) collective-permute-start(bf16[72,3072]{1,0:T(8,128)(2,1)S(1)} %collective-permute-done.8.refs_4_), channel_id=1, source_target_pairs={{0,6},{2,0},{4,2},{6,4},{1,7},{3,1},{5,3},{7,5},{8,14},{10,8},{12,... | collective-permute-start | bytes 1327112 | tf_op jit(solution)/shard_map/ppermute | solution.py:337
  43.7 9.6 %collective-permute-start.9 = (bf16[64,3072]{1,0:T(8,128)(2,1)}, bf16[64,3072]{1,0:T(8,128)(2,1)S(1)}, u32[]{:S(2)}, u32[]{:S(2)}) collective-permute-start(bf16[64,3072]{1,0:T(8,128)(2,1)} %collective-permute-done.6.refs_2_), channel_id=1, source_target_pairs={{0,2},{2,4},{4,6},{6,0},{1,3},{3,5},{5,7},{7,1},{8,10},{10,12},{12... | collective-permute-start | bytes 1179656 | tf_op jit(solution)/shard_map/ppermute | solution.py:337
  43.7 20.0 %collective-permute-start.5 = (bf16[72,3072]{1,0:T(8,128)(2,1)S(1)}, bf16[72,3072]{1,0:T(8,128)(2,1)}, u32[]{:S(2)}, u32[]{:S(2)}) collective-permute-start(bf16[72,3072]{1,0:T(8,128)(2,1)S(1)} %get-tuple-element.70), channel_id=1, source_target_pairs={{0,6},{2,0},{4,2},{6,4},{1,7},{3,1},{5,3},{7,5},{8,14},{10,8},{12,... | collective-permute-start | bytes 1327112 | tf_op jit(solution)/shard_map/ppermute | solution.py:337
  46.4 17.3 %collective-permute-start.4 = (bf16[64,3072]{1,0:T(8,128)(2,1)S(1)}, bf16[64,3072]{1,0:T(8,128)(2,1)}, u32[]{:S(2)}, u32[]{:S(2)}) collective-permute-start(bf16[64,3072]{1,0:T(8,128)(2,1)S(1)} %get-tuple-element.69), channel_id=1, source_target_pairs={{0,2},{2,4},{4,6},{6,0},{1,3},{3,5},{5,7},{7,1},{8,10},{10,12},{12... | collective-permute-start | bytes 1179656 | tf_op jit(solution)/shard_map/ppermute | solution.py:337
  47.1 28.2 %copy-start.32 = (s32[16]{0:T(128)}, s32[16]{0:T(128)S(1)}, u32[]{:S(2)}) copy-start(s32[16]{0:T(128)S(1)} %stack.76.order_ref) | copy-start | bytes 196
  54.1 21.2 %all-to-all-start = ((bf16[16,136,128]{2,1,0:T(8,128)(2,1)}), bf16[16,136,128]{2,1,0:T(8,128)(2,1)S(1)}, u32[]{:S(2)}, u32[]{:S(2)}) async-start(bf16[16,136,128]{2,1,0:T(8,128)(2,1)} %shard_map.155), calls=%async_computation | async-start | bytes 1114112 | tf_op jit(solution)/shard_map/all_to_all | solution.py:412
  71.5 3.2 %collective-permute-start.11 = (bf16[544,384]{1,0:T(8,128)(2,1)}, bf16[544,384]{1,0:T(8,128)(2,1)S(1)}, u32[]{:S(2)}, u32[]{:S(2)}) collective-permute-start(bf16[544,384]{1,0:T(8,128)(2,1)} %get-tuple-element.78), channel_id=1, source_target_pairs={{0,1},{1,0},{2,3},{3,2},{4,5},{5,4},{6,7},{7,6},{8,9},{9,8},{10,11... | collective-permute-start | bytes 1253384 | tf_op jit(solution)/shard_map/ppermute | solution.py:337
  73.1 2.2 %collective-permute-start.12 = (bf16[544,384]{1,0:T(8,128)(2,1)}, bf16[544,384]{1,0:T(8,128)(2,1)S(1)}, u32[]{:S(2)}, u32[]{:S(2)}) collective-permute-start(bf16[544,384]{1,0:T(8,128)(2,1)} %get-tuple-element.79), channel_id=1, source_target_pairs={{0,1},{1,0},{2,3},{3,2},{4,5},{5,4},{6,7},{7,6},{8,9},{9,8},{10,11... | collective-permute-start | bytes 1253384 | tf_op jit(solution)/shard_map/ppermute | solution.py:337
  98.3 5.4 %collective-permute-start.13 = (bf16[1088,384]{1,0:T(8,128)(2,1)}, bf16[1088,384]{1,0:T(8,128)(2,1)S(1)}, u32[]{:S(2)}, u32[]{:S(2)}) collective-permute-start(bf16[1088,384]{1,0:T(8,128)(2,1)} %get-tuple-element.83), channel_id=1, source_target_pairs={{0,1},{1,0},{2,3},{3,2},{4,5},{5,4},{6,7},{7,6},{8,9},{9,8},{10,11... | collective-permute-start | bytes 2506760 | tf_op jit(solution)/shard_map/ppermute | solution.py:337
  99.3 33.3 %all-to-all-start.1 = ((bf16[16,144,128]{2,1,0:T(8,128)(2,1)}), bf16[16,144,128]{2,1,0:T(8,128)(2,1)S(1)}, u32[]{:S(2)}, u32[]{:S(2)}) async-start(bf16[16,144,128]{2,1,0:T(8,128)(2,1)} %get-tuple-element.81), calls=%async_computation.1 | async-start | bytes 1179648 | tf_op jit(solution)/shard_map/all_to_all | solution.py:454
  111.1 37.2 %collective-permute-start.21 = (bf16[136,3072]{1,0:T(8,128)(2,1)}, bf16[136,3072]{1,0:T(8,128)(2,1)}, u32[]{:S(2)}, u32[]{:S(2)}) collective-permute-start(bf16[136,3072]{1,0:T(8,128)(2,1)} %get-tuple-element.84), channel_id=1, source_target_pairs={{0,8},{8,0},{1,9},{9,1},{2,10},{10,2},{3,11},{11,3},{4,12},{12,4},... | collective-permute-start | bytes 2506760 | tf_op jit(solution)/shard_map/ppermute | solution.py:337
  112.6 15.2 %collective-permute-start.15 = (bf16[64,3072]{1,0:T(8,128)(2,1)}, bf16[64,3072]{1,0:T(8,128)(2,1)S(1)}, u32[]{:S(2)}, u32[]{:S(2)}) collective-permute-start(bf16[64,3072]{1,0:T(8,128)(2,1)} %get-tuple-element.95), channel_id=1, source_target_pairs={{0,6},{2,0},{4,2},{6,4},{1,7},{3,1},{5,3},{7,5},{8,14},{10,8},{12,... | collective-permute-start | bytes 1179656 | tf_op jit(solution)/shard_map/ppermute | solution.py:337
  115.0 12.8 %collective-permute-start.16 = (bf16[72,3072]{1,0:T(8,128)(2,1)}, bf16[72,3072]{1,0:T(8,128)(2,1)S(1)}, u32[]{:S(2)}, u32[]{:S(2)}) collective-permute-start(bf16[72,3072]{1,0:T(8,128)(2,1)} %get-tuple-element.96), channel_id=1, source_target_pairs={{0,2},{2,4},{4,6},{6,0},{1,3},{3,5},{5,7},{7,1},{8,10},{10,12},{12... | collective-permute-start | bytes 1327112 | tf_op jit(solution)/shard_map/ppermute | solution.py:337
  115.0 12.8 %copy-start.22 = (bf16[144,3072]{1,0:T(8,128)(2,1)S(1)}, bf16[144,3072]{1,0:T(8,128)(2,1)}, u32[]{:S(2)}) copy-start(bf16[144,3072]{1,0:T(8,128)(2,1)} %get-tuple-element.94.two_ref) | copy-start | bytes 2654212
  115.0 12.8 %copy-start.23 = (bf16[128,3072]{1,0:T(8,128)(2,1)S(1)}, bf16[128,3072]{1,0:T(8,128)(2,1)}, u32[]{:S(2)}) copy-start(bf16[128,3072]{1,0:T(8,128)(2,1)} %get-tuple-element.93.one_ref) | copy-start | bytes 2359300
  126.8 5.8 %collective-permute-start.14 = (bf16[4,2,3,384,128]{4,3,2,1,0:T(8,128)(2,1)}, bf16[4,2,3,384,128]{4,3,2,1,0:T(8,128)(2,1)}, u32[]{:S(2)}, u32[]{:S(2)}) collective-permute-start(bf16[4,2,3,384,128]{4,3,2,1,0:T(8,128)(2,1)} %get-tuple-element.91), channel_id=1, source_target_pairs={{0,1},{1,0},{2,3},{3,2},{4,5},{5,4},{6,7},{7,6},{8,9},{9,8},{10,11... | collective-permute-start | bytes 7077896 | tf_op jit(solution)/shard_map/ppermute | solution.py:337
  129.6 20.2 %collective-permute-start.19 = (bf16[128,3072]{1,0:T(8,128)(2,1)}, bf16[128,3072]{1,0:T(8,128)(2,1)}, u32[]{:S(2)}, u32[]{:S(2)}) collective-permute-start(bf16[128,3072]{1,0:T(8,128)(2,1)} %get-tuple-element.97), channel_id=1, source_target_pairs={{0,6},{2,0},{4,2},{6,4},{1,7},{3,1},{5,3},{7,5},{8,14},{10,8},{12,... | collective-permute-start | bytes 2359304 | tf_op jit(solution)/shard_map/ppermute | solution.py:337
  132.6 22.5 %collective-permute-start.20 = (bf16[144,3072]{1,0:T(8,128)(2,1)}, bf16[144,3072]{1,0:T(8,128)(2,1)}, u32[]{:S(2)}, u32[]{:S(2)}) collective-permute-start(bf16[144,3072]{1,0:T(8,128)(2,1)} %get-tuple-element.98), channel_id=1, source_target_pairs={{0,2},{2,4},{4,6},{6,0},{1,3},{3,5},{5,7},{7,1},{8,10},{10,12},{12... | collective-permute-start | bytes 2654216 | tf_op jit(solution)/shard_map/ppermute | solution.py:337
  134.0 9.7 %collective-permute-start.17 = (bf16[1160,128]{1,0:T(8,128)(2,1)S(1)}, bf16[1160,128]{1,0:T(8,128)(2,1)S(1)}, u32[]{:S(2)}, u32[]{:S(2)}) collective-permute-start(bf16[1160,128]{1,0:T(8,128)(2,1)S(1)} %get-tuple-element.100), channel_id=1, source_target_pairs={{0,16},{16,32},{32,48},{48,0},{1,17},{17,33},{33,49},{49,1},{2,18}... | collective-permute-start | bytes 890888 | tf_op jit(solution)/shard_map/ppermute | solution.py:337
  135.3 8.4 %collective-permute-start.18 = (bf16[1160,128]{1,0:T(8,128)(2,1)S(1)}, bf16[1160,128]{1,0:T(8,128)(2,1)S(1)}, u32[]{:S(2)}, u32[]{:S(2)}) collective-permute-start(bf16[1160,128]{1,0:T(8,128)(2,1)S(1)} %get-tuple-element.101), channel_id=1, source_target_pairs={{0,48},{16,0},{32,16},{48,32},{1,49},{17,1},{33,17},{49,33},{2,50}... | collective-permute-start | bytes 890888 | tf_op jit(solution)/shard_map/ppermute | solution.py:337
  143.2 11.9 %copy-start.10 = (bf16[136,3072]{1,0:T(8,128)(2,1)S(1)}, bf16[136,3072]{1,0:T(8,128)(2,1)}, u32[]{:S(2)}) copy-start(bf16[136,3072]{1,0:T(8,128)(2,1)} %get-tuple-element.107.y_ref) | copy-start | bytes 2506756
  143.2 11.9 %copy-start.11 = (bf16[136,3072]{1,0:T(8,128)(2,1)S(1)}, bf16[136,3072]{1,0:T(8,128)(2,1)}, u32[]{:S(2)}) copy-start(bf16[136,3072]{1,0:T(8,128)(2,1)} %get-tuple-element.108.a_ref) | copy-start | bytes 2506756
  143.2 11.9 %copy-start.12 = (bf16[136,3072]{1,0:T(8,128)(2,1)S(1)}, bf16[136,3072]{1,0:T(8,128)(2,1)}, u32[]{:S(2)}) copy-start(bf16[136,3072]{1,0:T(8,128)(2,1)} %get-tuple-element.109.b_ref) | copy-start | bytes 2506756
  145.5 15.4 %collective-permute-start.22 = (bf16[2312,128]{1,0:T(8,128)(2,1)S(1)}, bf16[2312,128]{1,0:T(8,128)(2,1)S(1)}, u32[]{:S(2)}, u32[]{:S(2)}) collective-permute-start(bf16[2312,128]{1,0:T(8,128)(2,1)S(1)} %get-tuple-element.105), channel_id=1, source_target_pairs={{0,16},{16,32},{32,48},{48,0},{1,17},{17,33},{33,49},{49,1},{2,18}... | collective-permute-start | bytes 1775624 | tf_op jit(solution)/shard_map/ppermute | solution.py:337
  146.3 14.6 %collective-permute-start.23 = (bf16[2304,128]{1,0:T(8,128)(2,1)S(1)}, bf16[2304,128]{1,0:T(8,128)(2,1)S(1)}, u32[]{:S(2)}, u32[]{:S(2)}) collective-permute-start(bf16[2304,128]{1,0:T(8,128)(2,1)S(1)} %get-tuple-element.106), channel_id=1, source_target_pairs={{0,48},{16,0},{32,16},{48,32},{1,49},{17,1},{33,17},{49,33},{2,50}... | collective-permute-start | bytes 1769480 | tf_op jit(solution)/shard_map/ppermute | solution.py:337
  159.2 19.2 %collective-permute-start.24 = (bf16[136,3072]{1,0:T(8,128)(2,1)}, bf16[136,3072]{1,0:T(8,128)(2,1)S(1)}, u32[]{:S(2)}, u32[]{:S(2)}) collective-permute-start(bf16[136,3072]{1,0:T(8,128)(2,1)} %get-tuple-element.117), channel_id=1, source_target_pairs={{0,6},{2,0},{4,2},{6,4},{1,7},{3,1},{5,3},{7,5},{8,14},{10,8},{12,... | collective-permute-start | bytes 2506760 | tf_op jit(solution)/shard_map/ppermute | solution.py:337
  159.2 20.4 %collective-permute-start.25 = (bf16[136,3072]{1,0:T(8,128)(2,1)}, bf16[136,3072]{1,0:T(8,128)(2,1)S(1)}, u32[]{:S(2)}, u32[]{:S(2)}) collective-permute-start(bf16[136,3072]{1,0:T(8,128)(2,1)} %get-tuple-element.118), channel_id=1, source_target_pairs={{0,2},{2,4},{4,6},{6,0},{1,3},{3,5},{5,7},{7,1},{8,10},{10,12},{12... | collective-permute-start | bytes 2506760 | tf_op jit(solution)/shard_map/ppermute | solution.py:337
  160.7 18.9 %collective-permute-start.26 = (bf16[136,3072]{1,0:T(8,128)(2,1)}, bf16[136,3072]{1,0:T(8,128)(2,1)S(1)}, u32[]{:S(2)}, u32[]{:S(2)}) collective-permute-start(bf16[136,3072]{1,0:T(8,128)(2,1)} %get-tuple-element.110), channel_id=1, source_target_pairs={{0,8},{8,0},{1,9},{9,1},{2,10},{10,2},{3,11},{11,3},{4,12},{12,4},... | collective-permute-start | bytes 2506760 | tf_op jit(solution)/shard_map/ppermute | solution.py:337
  163.2 16.4 %copy-start.6 = (bf16[1,128,3072]{2,1,0:T(8,128)(2,1)S(1)}, bf16[1,128,3072]{2,1,0:T(8,128)(2,1)}, u32[]{:S(2)}) copy-start(bf16[1,128,3072]{2,1,0:T(8,128)(2,1)} %param.18) | copy-start | bytes 2359300
  163.2 16.4 %copy-start.8 = (bf16[1,128,3072]{2,1,0:T(8,128)(2,1)S(1)}, bf16[1,128,3072]{2,1,0:T(8,128)(2,1)}, u32[]{:S(2)}) copy-start(bf16[1,128,3072]{2,1,0:T(8,128)(2,1)} %param.10) | copy-start | bytes 2359300
  163.2 16.4 %copy-start.13 = (bf16[136,3072]{1,0:T(8,128)(2,1)S(1)}, bf16[136,3072]{1,0:T(8,128)(2,1)}, u32[]{:S(2)}) copy-start(bf16[136,3072]{1,0:T(8,128)(2,1)} %get-tuple-element.116.o_ref) | copy-start | bytes 2506756
  163.2 16.5 %copy-start.17 = (bf16[1,8,3072]{2,1,0:T(8,128)(2,1)S(1)}, bf16[1,8,3072]{2,1,0:T(8,128)(2,1)}, u32[]{:S(2)}) copy-start(bf16[1,8,3072]{2,1,0:T(8,128)(2,1)} %param.19) | copy-start | bytes 147460
  163.2 16.5 %copy-start.19 = (bf16[1,8,3072]{2,1,0:T(8,128)(2,1)S(1)}, bf16[1,8,3072]{2,1,0:T(8,128)(2,1)}, u32[]{:S(2)}) copy-start(bf16[1,8,3072]{2,1,0:T(8,128)(2,1)} %param.11) | copy-start | bytes 147460
  163.2 27.8 %collective-permute-start.27 = (bf16[1160,128]{1,0:T(8,128)(2,1)S(1)}, bf16[1160,128]{1,0:T(8,128)(2,1)S(1)}, u32[]{:S(2)}, u32[]{:S(2)}) collective-permute-start(bf16[1160,128]{1,0:T(8,128)(2,1)S(1)} %get-tuple-element.115), channel_id=1, source_target_pairs={{0,64},{64,0},{1,65},{65,1},{2,66},{66,2},{3,67},{67,3},{4,68},{68... | collective-permute-start | bytes 890888 | tf_op jit(solution)/shard_map/ppermute | solution.py:337
  180.3 10.7 %copy-start.15 = (f32[1152,128]{1,0:T(8,128)S(1)}, f32[1152,128]{1,0:T(8,128)}, u32[]{:S(2)}) copy-start(f32[1152,128]{1,0:T(8,128)} %copy-done.14) | copy-start | bytes 1769476
  183.2 16.3 %all-to-all-start.2 = ((bf16[16,3,3072]{2,1,0:T(4,128)(2,1)}), bf16[16,3,3072]{2,1,0:T(4,128)(2,1)S(1)}, u32[]{:S(2)}, u32[]{:S(2)}) async-start(bf16[16,3,3072]{2,1,0:T(4,128)(2,1)} %get-tuple-element.122), calls=%async_computation.2 | async-start | bytes 786432 | tf_op jit(solution)/shard_map/all_to_all | solution.py:574
  (16 other events, 39.5 us)

commit v2 on v1

--- a/solution.py
+++ b/solution.py
@@ -46,14 +46,11 @@
     return center * rstd, rstd
 
 
-def modulate_kernel(video_ref, text_ref, mod_ref, h_ref):
-    shift, scale = mod_ref[0:1, :], 1.0 + mod_ref[1:2, :]
+def norm_kernel(video_ref, text_ref, out_ref):
     vrows = video_ref.shape[0]
     for i in range(0, vrows, 16):
-        normed, _ = layer_norm(video_ref[i : i + 16, :].astype(F))
-        h_ref[i : i + 16, :] = (normed * scale + shift).astype(BF)
-    normed, _ = layer_norm(text_ref[...].astype(F))
-    h_ref[vrows:, :] = (normed * scale + shift).astype(BF)
+        out_ref[i : i + 16, :] = layer_norm(video_ref[i : i + 16, :].astype(F))[0].astype(BF)
+    out_ref[vrows:, :] = layer_norm(text_ref[...].astype(F))[0].astype(BF)
 
 
 def split_kernel(cut, y_ref, a_ref, b_ref, yt_ref, yl_ref, at_ref, bl_ref, m_ref):
@@ -67,10 +64,11 @@
 
 
 def qkv_kernel(pieces, *refs):
-    own_w, sib_w = refs[pieces : pieces + 2]
-    h_ref, own_ref, sib_ref, acc = refs[pieces + 2 :]
-    h = jnp.concatenate([ref[...] for ref in refs[:pieces]], axis=0)
-    h_ref[...] = h
+    own_w, sib_w, mod_ref = refs[pieces : pieces + 3]
+    n_ref, own_ref, sib_ref, acc = refs[pieces + 3 :]
+    normed = jnp.concatenate([ref[...] for ref in refs[:pieces]], axis=0)
+    n_ref[...] = normed
+    h = (normed.astype(F) * (1.0 + mod_ref[1:2, :]) + mod_ref[0:1, :]).astype(BF)
     w = side_by_side(own_w, sib_w)
     got = jnp.dot(h, w, preferred_element_type=F)
     step = pl.program_id(0)
@@ -121,11 +119,12 @@
     )
 
 
-def far_kernel(cut, own_ref, sib_ref, wo_ref, ws_ref, yct_ref, ycl_ref, m1_ref, m2_ref, m_ref):
+def far_kernel(cut, own_ref, sib_ref, wo_ref, ws_ref, yct_ref, ycl_ref, m1_ref, m2_ref, m_ref, sum_ref):
     d = jnp.concatenate([own_ref[...], sib_ref[...]], axis=1)
     w = side_by_side(wo_ref, ws_ref)
     got = lax.dot_general(d, w, NT, preferred_element_type=F)
     rows = got.shape[0] // 4
+    sum_ref[...] = jnp.sum(got, axis=0, keepdims=True)
     c, ya, yb, yc = (got[i * rows : (i + 1) * rows] for i in range(4))
     yct_ref[...] = yc[:cut].astype(BF)
     ycl_ref[...] = yc[cut:].astype(BF)
@@ -153,21 +152,35 @@
         out[...] = (ref[...].astype(F) + jnp.concatenate([top, low], axis=0)).astype(BF)
 
 
-def near_kernel(own_ref, sib_ref, wo_ref, ws_ref, o_ref, y_ref, a_ref, b_ref):
+def near_kernel(own_ref, sib_ref, wo_ref, ws_ref, o_ref, y_ref, a_ref, b_ref, sum_ref):
     d = jnp.concatenate([own_ref[...], sib_ref[...]], axis=1)
     w = side_by_side(wo_ref, ws_ref)
     got = lax.dot_general(d, w, NT, preferred_element_type=F)
     rows = got.shape[0] // 4
+    sum_ref[...] = jnp.sum(got, axis=0, keepdims=True)
     for i, ref in enumerate((o_ref, y_ref, a_ref, b_ref)):
         ref[...] = got[i * rows : (i + 1) * rows].astype(BF)
 
 
-def grad_w_kernel(place_ref, one_ref, two_ref, own_ref, sib_ref, own_out, sib_out):
-    h = jnp.concatenate([one_ref[...], two_ref[...]], axis=0)
+def grad_w_kernel(
+    place_ref, one_ref, two_ref, own_ref, sib_ref, wo_ref, ws_ref, mod_ref, own_out, sib_out, m_ref, total,
+):
     d = jnp.concatenate([own_ref[...], sib_ref[...]], axis=1)
-    got = lax.dot_general(h, d, TN, preferred_element_type=F)
+
+    @pl.when(pl.program_id(0) == 0)
+    def _():
+        total[...] = jnp.sum(d.astype(F), axis=0, keepdims=True)
+
+    normed = jnp.concatenate([one_ref[...], two_ref[...]], axis=0)
+    got = lax.dot_general(normed, d, TN, preferred_element_type=F)
+    w = side_by_side(wo_ref, ws_ref).astype(F)
+    prod = got * w
+    m_ref[...] = sum(prod[:, j : j + HD] for j in range(0, prod.shape[1], HD))
+    rows = jnp.concatenate([mod_ref[...], jnp.zeros((5, mod_ref.shape[1]), F)], axis=0)
+    columns = jnp.transpose(rows)
+    got = got * (1.0 + columns[:, 1:2]) + columns[:, 0:1] * total[...]
     wide, cols = own_out.shape[3], own_ref.shape[1]
-    count = h.shape[1] // wide
+    count = normed.shape[1] // wide
     for i in range(count):
         at = (lax.rem(pl.program_id(0) * count, 4) + i - place_ref[0]) % 4
         for j in range(3):
@@ -225,22 +238,13 @@
     sum_ref[...] = gains
 
 
-def tail_kernel(o_ref, ra_ref, rb_ref, ry_ref, video_ref, text_ref, dv_ref, dt_ref, mod_ref, dg_ref, gv_ref, gt_ref, m_ref):
+def tail_kernel(o_ref, ra_ref, rb_ref, ry_ref, video_ref, text_ref, dv_ref, dt_ref, mod_ref, gv_ref, gt_ref):
     scale = 1.0 + mod_ref[1:2, :]
     vrows = video_ref.shape[0]
-    first = jnp.zeros((8, scale.shape[1]), F)
-    second = first
-    everything = lambda at, n: (
-        o_ref[at : at + n, :].astype(F)
-        + ra_ref[at : at + n, :].astype(F)
-        + rb_ref[at : at + n, :].astype(F)
-        + ry_ref[at : at + n, :].astype(F)
-    )
-    fold = lambda v: jnp.sum(v.reshape(v.shape[0] // 8, 8, v.shape[1]), axis=0)
     pieces = [(i, 16, video_ref, dv_ref, gv_ref, i) for i in range(0, vrows, 16)]
     pieces.append((vrows, text_ref.shape[0], text_ref, dt_ref, gt_ref, 0))
     for at, n, x_ref, dy_ref, g_ref, lo in pieces:
-        d_h = everything(at, n)
+        d_h = sum(ref[at : at + n, :].astype(F) for ref in (o_ref, ra_ref, rb_ref, ry_ref))
         normed, rstd = layer_norm(x_ref[lo : lo + n, :].astype(F))
         t = d_h * scale
         back = rstd * (
@@ -249,11 +253,6 @@
             - normed * jnp.mean(t * normed, axis=-1, keepdims=True)
         )
         g_ref[lo : lo + n, :] = (dy_ref[lo : lo + n, :].astype(F) + back).astype(BF)
-        first += fold(d_h)
-        second += fold(d_h * normed)
-    rows = [jnp.sum(v, axis=0, keepdims=True) for v in (first, second)] + [dg_ref[...]]
-    m = jnp.concatenate(rows, axis=0).astype(BF)
-    m_ref[...] = jnp.broadcast_to(m[None], m_ref.shape)
 
 
 def rms(x):
@@ -360,7 +359,7 @@
     cut = 64
     part = rows - cut
 
-    h = call(modulate_kernel, shape((rows, width)))(video, text, modulation)
+    h = call(norm_kernel, shape((rows, width)))(video, text)
     w_own = jnp.transpose(w_qkv, (1, 0, 2))
     step = 2 * HD
     per = 4
@@ -398,14 +397,15 @@
             us=us,
             grid=(width // strip,),
             in_specs=[pl.BlockSpec((k.shape[0], strip), lambda i: (0, i)) for k in parts]
-            + [pl.BlockSpec((3, strip, HD), lambda i: (0, i, 0))] * 2,
+            + [pl.BlockSpec((3, strip, HD), lambda i: (0, i, 0))] * 2
+            + [pl.BlockSpec((3, strip), lambda i: (0, i))],
             out_specs=[
                 pl.BlockSpec((block, strip), lambda i: (0, i)),
                 whole((block, cols)),
                 whole((block, cols)),
             ],
             scratch_shapes=[pltpu.VMEM((block, 2 * cols), F)],
-        )(*parts, w_own, w_sib)
+        )(*parts, w_own, w_sib, modulation)
 
     h_one, own_one, sib_one = project(0, h, h_y, h_a, h_b)
     yc_t, yc_l = zp(tie(ya_t, own_one)), zm(tie(yb_l, own_one))
@@ -461,40 +461,36 @@
         pl.BlockSpec((3, strip, HD), lambda i: (0, i, 0)),
     ]
     work = dict(grid=(width // strip,), mib=56)
-    yc_t, yc_l, m_1, m_2, m_3 = call(
+    yc_t, yc_l, m_1, m_2, m_3, far_sum = call(
         functools.partial(far_kernel, cut),
-        tuple(shape((k, width)) for k in sizes),
+        tuple(shape((k, width)) for k in sizes) + (shape((1, width), F),),
         in_specs=half_specs(1),
-        out_specs=[strips(k) for k in sizes],
+        out_specs=[strips(k) for k in sizes + (1,)],
         **work,
     )(d_own, d_sib, w_own, w_sib)
     r_ya, r_yb = zm(yc_t), zp(yc_l)
     r_3 = yy(m_3)
-    g_own, g_sib = call(
+    g_own, g_sib, mod_sums = call(
         grad_w_kernel,
-        (shape((4, 2, 3, wide, HD)),) * 2,
+        (shape((4, 2, 3, wide, HD)),) * 2 + (shape((width, HD), F),),
         us=20,
         mib=56,
         grid_spec=pltpu.PrefetchScalarGridSpec(
             num_scalar_prefetch=1,
             grid=(4,),
             in_specs=[pl.BlockSpec((block, 2 * wide), lambda i, p: (0, i))] * 2
-            + [whole((n, cols))] * 2,
+            + [whole((n, cols))] * 2
+            + [pl.BlockSpec((3, 2 * wide, HD), lambda i, p: (0, i, 0))] * 2
+            + [pl.BlockSpec((3, 2 * wide), lambda i, p: (0, i))],
             out_specs=[
                 pl.BlockSpec((4, 1, 3, wide, HD), lambda i, p: (0, (i // 2 - p[1]) % 2, 0, 0, 0))
             ]
-            * 2,
+            * 2
+            + [pl.BlockSpec((2 * wide, HD), lambda i, p: (i, 0))],
+            scratch_shapes=[pltpu.VMEM((1, 2 * cols), F)],
         ),
-    )(tie(here, m_3), h_one, h_two, d_own, d_sib)
-
-    p_o, p_y, p_a, p_b = call(
-        near_kernel,
-        (shape((rows, width)),) * 4,
-        in_specs=half_specs(0),
-        out_specs=[strips(rows)] * 4,
-        us=30,
-        **work,
-    )(tie(d_own, m_3), d_sib, w_own, w_sib)
+    )(tie(here, m_3), h_one, h_two, d_own, d_sib, w_own, w_sib, modulation)
+
 
     thirds = lambda count: pl.BlockSpec((count, width // 3), lambda i: (0, i))
 
@@ -519,6 +515,14 @@
         out_specs=[whole((flat + 8, HD)), whole((flat + 8, HD)), whole((2, HD))],
     )(g_own, g_got, tie(attn_tok, m_1, m_2))
     got_b, got_a = ring(far_0, "x", -1), ring(far_1, "x", 1)
+    p_o, p_y, p_a, p_b, near_sum = call(
+        near_kernel,
+        (shape((rows, width)),) * 4 + (shape((1, width), F),),
+        in_specs=half_specs(0),
+        out_specs=[strips(rows)] * 4 + [strips(1)],
+        us=30,
+        **work,
+    )(tie(d_own, m_3, far_0), d_sib, w_own, w_sib)
     send_a, send_b, gains = call(
         near_section_kernel,
         (shape((2 * flat + 8, HD)), shape((2 * flat, HD)), two),
@@ -566,12 +570,18 @@
         scratch_shapes=[pltpu.VMEM((rows, heads * HD), BF)],
     )(tie(attn_tok, p_y), w_out, video, text, cot_video, cot_text, gate)
 
-    grad_video, grad_text, wide_mod = call(
+    mod_sums = jnp.sum(tie(mod_sums, p_y), axis=1)[None]
+    mod_sums = jnp.concatenate([far_sum + near_sum, mod_sums, d_gate], axis=0).astype(BF)
+    wide_mod = jnp.broadcast_to(mod_sums[None], (heads,) + mod_sums.shape)
+    grad_video, grad_text = call(
         tail_kernel,
-        (shape((vrows, width)), shape((trows, width)), shape((heads, 3, width))),
-    )(tie(p_o, give), last_a, last_b, last_y, video, text, cot_video, cot_text, modulation, d_gate)
+        (shape((vrows, width)), shape((trows, width))),
+    )(tie(p_o, give), last_a, last_b, last_y, video, text, cot_video, cot_text, modulation)
     grad_mod = jnp.sum(
-        lax.all_to_all(wide_mod, SEQ, split_axis=0, concat_axis=0, tiled=True).astype(F), axis=0
+        tie(
+            lax.all_to_all(wide_mod, SEQ, split_axis=0, concat_axis=0, tiled=True), grad_video
+        ).astype(F),
+        axis=0,
     )
     return (
         out_video[None],

time: 202 us -> 198 us (0.980)
  waiting for transfers between devices: 37.6 us -> 25.8 us
  Pallas kernels: 94.4 us -> 98.9 us
  other arithmetic: 2.28 us -> 6.64 us
  starting transfers between devices: 54.5 us -> 51 us
  local copies, waits for them, and re-layouts: 9.9 us -> 12.5 us
    all_to_all x1, waiting for transfers between devices: 7.02 us -> 0.01 us  [per_device(): lax.all_to_all(wide_mod, SEQ, split_axis=0, concat_axis=0, tiled=True)]
    ppermute x28, waiting for transfers between devices: 30.6 us -> 25.8 us  [ring(): lax.ppermute(values, axis, [(i, (i + distance) % size) for i in range(siz...]
    pallas_call x4, Pallas kernels: 21.7 us -> 24.9 us  [the longest x1 14.1 us: per_device(): call(grad_w_kernel, (shape((4, 2, 3, wide, HD)),) * 2 + (shape((width, HD...]
    reduce_sum x1 -> x2, other arithmetic: 0.17 us -> 3.06 us  [the longest x1 1.89 us: per_device(): mod_sums = jnp.sum(tie(mod_sums, p_y), axis=1)[None]]
    unnamed x67 -> x72, local copies, waits for them, and re-layouts: 7.74 us -> 10.1 us
  transfers between devices with their start and end apart: 31 -> 31, of which waited for: 13 -> 10; matrix products, arithmetic and copies ran while one was open for 2% -> 5% of each run, Pallas kernels for 36% -> 39%
where the time goes in v2:
time: 198 us; the launch traced here: 197 us
  Pallas kernels  98.9 us (50%)
  starting transfers between devices  51 us (26%)
  waiting for transfers between devices  25.8 us (13%)
  local copies, waits for them, and re-layouts  12.5 us (6%)
  other arithmetic  6.64 us (3%)
    ppermute x28, starting transfers between devices, ring(): lax.ppermute(values, axis, [(i, (i + distance) % size) for i in range(siz...  31.1 us
    ppermute x28, waiting for transfers between devices, ring(): lax.ppermute(values, axis, [(i, (i + distance) % size) for i in range(siz...  25.8 us
    pallas_call x1, Pallas kernels, per_device(): call(functools.partial(attn_kernel, rows), (shape((heads, rows + 8, HD)),...  22.1 us
    pallas_call x2, Pallas kernels, project(): call(functools.partial(qkv_kernel, len(parts)), (shape((block, width)), s...  15.4 us
    pallas_call x1, Pallas kernels, per_device(): call(grad_w_kernel, (shape((4, 2, 3, wide, HD)),) * 2 + (shape((width, HD...  14.1 us
    pallas_call x1, Pallas kernels, per_device(): call(d_attn_kernel, shape((heads, rows, HD)), grid=(2 * per,), in_specs=[...  10.2 us
    unnamed x72, local copies, waits for them, and re-layouts  10.1 us
    all_to_all x1, starting transfers between devices, per_device(): lax.all_to_all(tie(d_attn, yc_t, yc_l), SEQ, split_axis=0, concat_axis=0,...  9.45 us
  transfers between devices with their start and end apart: 31, of which 10 were waited for; matrix products, arithmetic and copies ran while one was open for 5% of the time, Pallas kernels for 39%

profile of v2, /device:TPU:1, one launch (start us, length us, event | category | flops | bytes accessed | tf_op | source)
XLA Modules:
  0.0 196.6 jit_solution(5867197893241513045)
XLA Ops:
  0.6 1.5 collective-permute-start.3
  2.1 1.1 copy-done.7
  3.3 0.8 copy-done.19
  4.6 1.5 collective-permute-start
  6.0 3.8 %collective-permute-start.2 = (bf16[136,3072]{1,0:T(8,128)(2,1)S(1)}, bf16[136,3072]{1,0:T(8,128)(2,1)S(1)}, u32[]{:S(2)}, u32[]{:S(2)}) collective-permute-start(bf16[136,3072]{1,0:T(8,128)(2,1)S(1)} %shard_map.153.refs_0_), channel_id=1, source_target_pairs={{0,6},{2,0},{4,2},{6,4},{1,7},{3,1},{5,3},{7,5},{8,14},{10,8},{12,... | collective-permute-start | bytes 2506760 | tf_op jit(solution)/shard_map/ppermute | solution.py:336
  10.5 1.7 copy-done.5
  13.0 10.2 %shard_map.155 = bf16[16,136,128]{2,1,0:T(8,128)(2,1)} custom-call(bf16[128,3072]{1,0:T(8,128)(2,1)S(1)} %bitcast.41, bf16[8,3072]{1,0:T(8,128)(2,1)S(1)} %bitcast.51, f32[1,3072]{1,0:T(1,128)S(1)} %slice_bitcast_fusion.gate_ref, bf16[2048,3072]{1,0:T(8,128)(2,1)} %w_ref.3), custom_call_target="tpu_custom_call" | custom-call | flops 1 | bytes 1 | tf_op jit(solution)/shard_map/pallas_call | solution.py:369
  23.2 1.6 collective-permute-done.refs_1_.y_ref
  24.9 2.6 %collective-permute-done.2.refs_3_.b_ref = bf16[136,3072]{1,0:T(8,128)(2,1)S(1)} collective-permute-done((bf16[136,3072]{1,0:T(8,128)(2,1)S(1)}, bf16[136,3072]{1,0:T(8,128)(2,1)S(1)}, u32[]{:S(2)}, u32[]{:S(2)}) %collective-permute-start.2) | collective-permute-done | bytes 835616 | tf_op jit(solution)/shard_map/ppermute | solution.py:336
  27.5 3.1 %collective-permute-done.1.refs_2_.a_ref = bf16[136,3072]{1,0:T(8,128)(2,1)S(1)} collective-permute-done((bf16[136,3072]{1,0:T(8,128)(2,1)S(1)}, bf16[136,3072]{1,0:T(8,128)(2,1)S(1)}, u32[]{:S(2)}, u32[]{:S(2)}) %collective-permute-start.1) | collective-permute-done | bytes 835616 | tf_op jit(solution)/shard_map/ppermute | solution.py:336
  31.2 1.1 collective-permute-start.6
  33.1 7.7 %shard_map.154 = (bf16[544,3072]{1,0:T(8,128)(2,1)}, bf16[544,384]{1,0:T(8,128)(2,1)}, bf16[544,384]{1,0:T(8,128)(2,1)}) custom-call(bf16[136,3072]{1,0:T(8,128)(2,1)} %copy-done.4, bf16[136,3072]{1,0:T(8,128)(2,1)} %copy-done.1, bf16[136,3072]{1,0:T(8,128)(2,1)} %copy-done.3, bf16[136,3072]{1,0:T(8,128)(2,1)} %copy-done.2, bf16[3,3072,128]{2,1,0:T(8,128)(2,1)} %bitcast.57, ...), custom_call_target="tpu_custom_call" | custom-call | flops 1 | bytes 1 | tf_op jit(solution)/shard_map/pallas_call | solution.py:393
  41.1 1.8 collective-permute-start.10
  42.9 2.7 %collective-permute-start.5 = (bf16[72,3072]{1,0:T(8,128)(2,1)S(1)}, bf16[72,3072]{1,0:T(8,128)(2,1)}, u32[]{:S(2)}, u32[]{:S(2)}) collective-permute-start(bf16[72,3072]{1,0:T(8,128)(2,1)S(1)} %get-tuple-element.74), channel_id=1, source_target_pairs={{0,6},{2,0},{4,2},{6,4},{1,7},{3,1},{5,3},{7,5},{8,14},{10,8},{12,... | collective-permute-start | bytes 1327112 | tf_op jit(solution)/shard_map/ppermute | solution.py:336
  46.4 6.4 %collective-permute-done.9.refs_5_ = bf16[64,3072]{1,0:T(8,128)(2,1)} collective-permute-done((bf16[64,3072]{1,0:T(8,128)(2,1)}, bf16[64,3072]{1,0:T(8,128)(2,1)}, u32[]{:S(2)}, u32[]{:S(2)}) %collective-permute-start.9) | collective-permute-done | bytes 393248 | tf_op jit(solution)/shard_map/ppermute | solution.py:336
  53.5 9.5 %all-to-all-start = ((bf16[16,136,128]{2,1,0:T(8,128)(2,1)}), bf16[16,136,128]{2,1,0:T(8,128)(2,1)S(1)}, u32[]{:S(2)}, u32[]{:S(2)}) async-start(bf16[16,136,128]{2,1,0:T(8,128)(2,1)} %shard_map.155), calls=%async_computation | async-start | bytes 1114112 | tf_op jit(solution)/shard_map/all_to_all | solution.py:412
  63.0 0.9 copy-done.27
  63.9 7.8 %shard_map.157 = (bf16[544,3072]{1,0:T(8,128)(2,1)}, bf16[544,384]{1,0:T(8,128)(2,1)}, bf16[544,384]{1,0:T(8,128)(2,1)}) custom-call(bf16[64,3072]{1,0:T(8,128)(2,1)} %collective-permute-done.4.refs_0_, bf16[72,3072]{1,0:T(8,128)(2,1)} %collective-permute-done.5.refs_1_, bf16[64,3072]{1,0:T(8,128)(2,1)} %collective-permute-done.6.refs_2_, ...), custom_call_target="tpu_custom_call" | custom-call | flops 1 | bytes 1 | tf_op jit(solution)/shard_map/pallas_call | solution.py:393
  71.7 1.5 collective-permute-start.11
  76.3 22.1 %shard_map.158 = (bf16[16,144,128]{2,1,0:T(8,128)(2,1)}, bf16[1088,384]{1,0:T(8,128)(2,1)}, bf16[1088,384]{1,0:T(8,128)(2,1)}) custom-call(s32[16]{0:T(128)} %copy-done.34, bf16[544,384]{1,0:T(8,128)(2,1)} %get-tuple-element.70.q1_ref, bf16[544,384]{1,0:T(8,128)(2,1)} %get-tuple-element.80.q2_ref, bf16[544,384]{1,0:T(8,128)(2,1)} %copy-done.30, ...), custom_call_target="tpu_custom_call" | custom-call | flops 1 | bytes 1 | tf_op jit(solution)/shard_map/pallas_call | solution.py:426
  99.3 4.5 %all-to-all-start.1 = ((bf16[16,144,128]{2,1,0:T(8,128)(2,1)}), bf16[16,144,128]{2,1,0:T(8,128)(2,1)S(1)}, u32[]{:S(2)}, u32[]{:S(2)}) async-start(bf16[16,144,128]{2,1,0:T(8,128)(2,1)} %get-tuple-element.85), calls=%async_computation.1 | async-start | bytes 1179648 | tf_op jit(solution)/shard_map/all_to_all | solution.py:454
  103.9 0.9 copy-done.26
  104.8 6.4 %shard_map.159 = (bf16[64,3072]{1,0:T(8,128)(2,1)}, bf16[72,3072]{1,0:T(8,128)(2,1)}, bf16[128,3072]{1,0:T(8,128)(2,1)}, bf16[144,3072]{1,0:T(8,128)(2,1)}, bf16...) custom-call(bf16[1088,384]{1,0:T(8,128)(2,1)} %get-tuple-element.103.own_ref, bf16[1088,384]{1,0:T(8,128)(2,1)} %copy-done.26, ...), custom_call_target="tpu_custom_call" | custom-call | flops 1 | bytes 1 | tf_op jit(solution)/shard_map/pallas_call | solution.py:464
  111.2 1.5 collective-permute-start.21
  112.7 2.4 %collective-permute-start.15 = (bf16[64,3072]{1,0:T(8,128)(2,1)}, bf16[64,3072]{1,0:T(8,128)(2,1)S(1)}, u32[]{:S(2)}, u32[]{:S(2)}) collective-permute-start(bf16[64,3072]{1,0:T(8,128)(2,1)} %get-tuple-element.97), channel_id=1, source_target_pairs={{0,6},{2,0},{4,2},{6,4},{1,7},{3,1},{5,3},{7,5},{8,14},{10,8},{12,... | collective-permute-start | bytes 1179656 | tf_op jit(solution)/shard_map/ppermute | solution.py:336
  115.1 14.1 %shard_map.160 = (bf16[4,2,3,384,128]{4,3,2,1,0:T(8,128)(2,1)}, bf16[4,2,3,384,128]{4,3,2,1,0:T(8,128)(2,1)}, f32[3072,128]{1,0:T(8,128)}) custom-call(s32[2]{0:T(128)} %pad_add_fusion.place_ref, bf16[544,3072]{1,0:T(8,128)(2,1)} %get-tuple-element.90.one_ref, bf16[544,3072]{1,0:T(8,128)(2,1)} %get-tuple-element.91.two_ref, ...), custom_call_target="tpu_custom_call" | custom-call | flops 22000001024 | bytes 1 | tf_op jit(solution)/shard_map/pallas_call | solution.py:473
  129.3 0.9 collective-permute-start.14
  130.2 1.9 shard_map.161
  132.1 3.0 %collective-permute-start.19 = (bf16[128,3072]{1,0:T(8,128)(2,1)}, bf16[128,3072]{1,0:T(8,128)(2,1)}, u32[]{:S(2)}, u32[]{:S(2)}) collective-permute-start(bf16[128,3072]{1,0:T(8,128)(2,1)} %get-tuple-element.99), channel_id=1, source_target_pairs={{0,6},{2,0},{4,2},{6,4},{1,7},{3,1},{5,3},{7,5},{8,14},{10,8},{12,... | collective-permute-start | bytes 2359304 | tf_op jit(solution)/shard_map/ppermute | solution.py:336
  135.1 1.4 shard_map.162
  136.5 2.5 %collective-permute-start.18 = (bf16[1160,128]{1,0:T(8,128)(2,1)S(1)}, bf16[1160,128]{1,0:T(8,128)(2,1)S(1)}, u32[]{:S(2)}, u32[]{:S(2)}) collective-permute-start(bf16[1160,128]{1,0:T(8,128)(2,1)S(1)} %get-tuple-element.102), channel_id=1, source_target_pairs={{0,48},{16,0},{32,16},{48,32},{1,49},{17,1},{33,17},{49,33},{2,50}... | collective-permute-start | bytes 890888 | tf_op jit(solution)/shard_map/ppermute | solution.py:336
  139.1 6.5 %shard_map.163 = (bf16[136,3072]{1,0:T(8,128)(2,1)}, bf16[136,3072]{1,0:T(8,128)(2,1)}, bf16[136,3072]{1,0:T(8,128)(2,1)}, bf16[136,3072]{1,0:T(8,128)(2,1)}, f32[1,3072]{1,0:T(1,128)}) custom-call(bf16[1088,384]{1,0:T(8,128)(2,1)} %get-tuple-element.103.own_ref, bf16[1088,384]{1,0:T(8,128)(2,1)} %copy-done.26, bf16[3,3072,128]{2,1,0:T(8,128)(2,1)} %bitcast.61, ...), custom_call_target="tpu_custom_call" | custom-call | flops 32999999488 | bytes 1 | tf_op jit(solution)/shard_map/pallas_call | solution.py:518
  146.3 2.1 %collective-permute-done.17.ga_ref = bf16[1160,128]{1,0:T(8,128)(2,1)S(1)} collective-permute-done((bf16[1160,128]{1,0:T(8,128)(2,1)S(1)}, bf16[1160,128]{1,0:T(8,128)(2,1)S(1)}, u32[]{:S(2)}, u32[]{:S(2)}) %collective-permute-start.17) | collective-permute-done | bytes 296992 | tf_op jit(solution)/shard_map/ppermute | solution.py:336
  148.4 2.4 %shard_map.164 = (bf16[2312,128]{1,0:T(8,128)(2,1)}, bf16[2304,128]{1,0:T(8,128)(2,1)}, f32[2,128]{1,0:T(2,128)S(1)}) custom-call(bf16[4,2,3,384,128]{4,3,2,1,0:T(8,128)(2,1)S(1)} %copy-done, bf16[4,2,3,384,128]{4,3,2,1,0:T(8,128)(2,1)} %collective-permute-done.14.got_ref.ag_ref.bg_ref, bf16[4,2,3,384,128]{4,3,2,1,0:T(8,128)(2,1)S(1)} %copy-done, ...), custom_call_target="tpu_custom_call" | custom-call | flops 1 | bytes 1 | tf_op jit(solution)/shard_map/pallas_call | solution.py:526
  152.3 5.2 %collective-permute-done.20.r2_ref = bf16[144,3072]{1,0:T(8,128)(2,1)} collective-permute-done((bf16[144,3072]{1,0:T(8,128)(2,1)}, bf16[144,3072]{1,0:T(8,128)(2,1)}, u32[]{:S(2)}, u32[]{:S(2)}) %collective-permute-start.20) | collective-permute-done | bytes 884768 | tf_op jit(solution)/shard_map/ppermute | solution.py:336
  157.5 4.1 %shard_map.165 = (bf16[136,3072]{1,0:T(8,128)(2,1)}, bf16[136,3072]{1,0:T(8,128)(2,1)}, bf16[136,3072]{1,0:T(8,128)(2,1)}) custom-call(bf16[136,3072]{1,0:T(8,128)(2,1)S(1)} %copy-done.11, bf16[136,3072]{1,0:T(8,128)(2,1)S(1)} %copy-done.12, bf16[136,3072]{1,0:T(8,128)(2,1)S(1)} %copy-done.13, bf16[128,3072]{1,0:T(8,128)(2,1)} %collective-permute-done.19.r1_ref, ...), custom_call_target="tpu_custom_call" | custom-call | flops 1 | bytes 1 | tf_op jit(solution)/shard_map/pallas_call | solution.py:533
  162.0 1.5 collective-permute-start.25
  163.4 7.9 %shard_map.166 = (bf16[128,3072]{1,0:T(8,128)(2,1)}, bf16[8,3072]{1,0:T(8,128)(2,1)}, f32[1,3072]{1,0:T(1,128)}) custom-call(bf16[16,144,128]{2,1,0:T(8,128)(2,1)} %copy-done.9, bf16[2048,3072]{1,0:T(8,128)(2,1)} %w_ref.3, bf16[128,3072]{1,0:T(8,128)(2,1)} %bitcast.43, bf16[8,3072]{1,0:T(8,128)(2,1)} %bitcast.53, bf16[128,3072]{1,0:T(8,128)(2,1)} %bitcast.40, ...), custom_call_target="tpu_custom_call" | custom-call | flops 8800000000 | bytes 1 | tf_op jit(solution)/shard_map/pallas_call | solution.py:558
  171.4 1.9 reduce_sum.18
  174.1 0.8 broadcast_in_dim.46
  174.9 5.9 %all-to-all-start.2 = ((bf16[16,3,3072]{2,1,0:T(4,128)(2,1)}), bf16[16,3,3072]{2,1,0:T(4,128)(2,1)}, u32[]{:S(2)}, u32[]{:S(2)}) async-start(bf16[16,3,3072]{2,1,0:T(4,128)(2,1)} %broadcast_in_dim.46), calls=%async_computation.2 | async-start | bytes 786432 | tf_op jit(solution)/shard_map/all_to_all | solution.py:582
  180.9 1.9 shard_map.167
  182.8 0.8 copy-done.15
  183.6 2.6 %collective-permute-start.27 = (bf16[1160,128]{1,0:T(8,128)(2,1)S(1)}, bf16[1160,128]{1,0:T(8,128)(2,1)S(1)}, u32[]{:S(2)}, u32[]{:S(2)}) collective-permute-start(bf16[1160,128]{1,0:T(8,128)(2,1)S(1)} %get-tuple-element.119), channel_id=1, source_target_pairs={{0,64},{64,0},{1,65},{65,1},{2,66},{66,2},{3,67},{67,3},{4,68},{68... | collective-permute-start | bytes 890888 | tf_op jit(solution)/shard_map/ppermute | solution.py:336
  186.2 3.8 %shard_map.168 = (bf16[128,3072]{1,0:T(8,128)(2,1)}, bf16[8,3072]{1,0:T(8,128)(2,1)}) custom-call(bf16[136,3072]{1,0:T(8,128)(2,1)S(1)} %copy-done.10, bf16[136,3072]{1,0:T(8,128)(2,1)} %collective-permute-done.24.ra_ref, bf16[136,3072]{1,0:T(8,128)(2,1)} %collective-permute-done.25.rb_ref, bf16[136,3072]{1,0:T(8,128)(2,1)S(1)} %collective-permute-done.26.ry_ref, ...), custom_call_target="tpu_custom_call" | custom-call | flops 1 | bytes 1 | tf_op jit(solution)/shard_map/pallas_call | solution.py:576
  190.1 1.2 convert_reduce_fusion
  191.9 3.2 %collective-permute-done.27 = bf16[1160,128]{1,0:T(8,128)(2,1)S(1)} collective-permute-done((bf16[1160,128]{1,0:T(8,128)(2,1)S(1)}, bf16[1160,128]{1,0:T(8,128)(2,1)S(1)}, u32[]{:S(2)}, u32[]{:S(2)}) %collective-permute-start.27) | collective-permute-done | bytes 296992 | tf_op jit(solution)/shard_map/ppermute | solution.py:336
  195.7 0.9 convert_add_fusion
  (119 shorter events, 13.4 us)
Async XLA Ops:
  0.6 9.9 %collective-permute-start.3 = (bf16[3,3072,128]{2,1,0:T(8,128)(2,1)}, bf16[3,3072,128]{2,1,0:T(8,128)(2,1)S(1)}, u32[]{:S(2)}, u32[]{:S(2)}) collective-permute-start(bf16[3,3072,128]{2,1,0:T(8,128)(2,1)} %bitcast.56), channel_id=1, source_target_pairs={{0,1},{1,0},{2,3},{3,2},{4,5},{5,4},{6,7},{7,6},{8,9},{9,8},{10,11... | collective-permute-start | bytes 7077896 | tf_op jit(solution)/shard_map/ppermute | solution.py:336
  4.6 18.6 %copy-start.4 = (bf16[136,3072]{1,0:T(8,128)(2,1)}, bf16[136,3072]{1,0:T(8,128)(2,1)S(1)}, u32[]{:S(2)}) copy-start(bf16[136,3072]{1,0:T(8,128)(2,1)S(1)} %shard_map.153.refs_0_) | copy-start | bytes 2506756
  4.6 20.3 %collective-permute-start = (bf16[136,3072]{1,0:T(8,128)(2,1)S(1)}, bf16[136,3072]{1,0:T(8,128)(2,1)S(1)}, u32[]{:S(2)}, u32[]{:S(2)}) collective-permute-start(bf16[136,3072]{1,0:T(8,128)(2,1)S(1)} %shard_map.153.refs_0_), channel_id=1, source_target_pairs={{0,8},{8,0},{1,9},{9,1},{2,10},{10,2},{3,11},{11,3},{4,12},{12,4},... | collective-permute-start | bytes 2506760 | tf_op jit(solution)/shard_map/ppermute | solution.py:336
  6.0 21.4 %collective-permute-start.2 = (bf16[136,3072]{1,0:T(8,128)(2,1)S(1)}, bf16[136,3072]{1,0:T(8,128)(2,1)S(1)}, u32[]{:S(2)}, u32[]{:S(2)}) collective-permute-start(bf16[136,3072]{1,0:T(8,128)(2,1)S(1)} %shard_map.153.refs_0_), channel_id=1, source_target_pairs={{0,6},{2,0},{4,2},{6,4},{1,7},{3,1},{5,3},{7,5},{8,14},{10,8},{12,... | collective-permute-start | bytes 2506760 | tf_op jit(solution)/shard_map/ppermute | solution.py:336
  9.8 20.8 %collective-permute-start.1 = (bf16[136,3072]{1,0:T(8,128)(2,1)S(1)}, bf16[136,3072]{1,0:T(8,128)(2,1)S(1)}, u32[]{:S(2)}, u32[]{:S(2)}) collective-permute-start(bf16[136,3072]{1,0:T(8,128)(2,1)S(1)} %shard_map.153.refs_0_), channel_id=1, source_target_pairs={{0,2},{2,4},{4,6},{6,0},{1,3},{3,5},{5,7},{7,1},{8,10},{10,12},{12... | collective-permute-start | bytes 2506760 | tf_op jit(solution)/shard_map/ppermute | solution.py:336
  10.5 12.7 %copy-start.21 = (f32[1,3072]{1,0:T(1,128)}, f32[1,3072]{1,0:T(1,128)S(1)}, u32[]{:S(2)}) copy-start(f32[1,3072]{1,0:T(1,128)S(1)} %slice_bitcast_fusion.gate_ref) | copy-start | bytes 36868
  10.5 12.7 %copy-start.24 = (bf16[3,3072,128]{2,1,0:T(8,128)(2,1)}, bf16[3,3072,128]{2,1,0:T(8,128)(2,1)S(1)}, u32[]{:S(2)}) copy-start(bf16[3,3072,128]{2,1,0:T(8,128)(2,1)S(1)} %collective-permute-done.3.refs_5_.refs_8_.ws_ref) | copy-start | bytes 7077892
  23.2 9.2 %copy-start.32 = (f32[1,3,3072]{2,0,1:T(1,128)S(1)}, f32[1,3,3072]{2,0,1:T(1,128)}, u32[]{:S(2)}) copy-start(f32[1,3,3072]{2,0,1:T(1,128)} %param.13) | copy-start | bytes 110596
  24.9 8.2 %copy-start.1 = (bf16[136,3072]{1,0:T(8,128)(2,1)}, bf16[136,3072]{1,0:T(8,128)(2,1)S(1)}, u32[]{:S(2)}) copy-start(bf16[136,3072]{1,0:T(8,128)(2,1)S(1)} %collective-permute-done.refs_1_.y_ref) | copy-start | bytes 2506756
  27.5 5.6 %copy-start.2 = (bf16[136,3072]{1,0:T(8,128)(2,1)}, bf16[136,3072]{1,0:T(8,128)(2,1)S(1)}, u32[]{:S(2)}) copy-start(bf16[136,3072]{1,0:T(8,128)(2,1)S(1)} %collective-permute-done.2.refs_3_.b_ref) | copy-start | bytes 2506756
  30.8 10.4 %collective-permute-start.8 = (bf16[72,3072]{1,0:T(8,128)(2,1)S(1)}, bf16[72,3072]{1,0:T(8,128)(2,1)S(1)}, u32[]{:S(2)}, u32[]{:S(2)}) collective-permute-start(bf16[72,3072]{1,0:T(8,128)(2,1)S(1)} %get-tuple-element.77), channel_id=1, source_target_pairs={{0,6},{2,0},{4,2},{6,4},{1,7},{3,1},{5,3},{7,5},{8,14},{10,8},{12,... | collective-permute-start | bytes 1327112 | tf_op jit(solution)/shard_map/ppermute | solution.py:336
  31.2 11.8 %collective-permute-start.6 = (bf16[64,3072]{1,0:T(8,128)(2,1)S(1)}, bf16[64,3072]{1,0:T(8,128)(2,1)}, u32[]{:S(2)}, u32[]{:S(2)}) collective-permute-start(bf16[64,3072]{1,0:T(8,128)(2,1)S(1)} %get-tuple-element.75), channel_id=1, source_target_pairs={{0,2},{2,4},{4,6},{6,0},{1,3},{3,5},{5,7},{7,1},{8,10},{10,12},{12... | collective-permute-start | bytes 1179656 | tf_op jit(solution)/shard_map/ppermute | solution.py:336
  32.3 30.7 %collective-permute-start.7 = (bf16[136,3072]{1,0:T(8,128)(2,1)S(1)}, bf16[136,3072]{1,0:T(8,128)(2,1)S(1)}, u32[]{:S(2)}, u32[]{:S(2)}) collective-permute-start(bf16[136,3072]{1,0:T(8,128)(2,1)S(1)} %get-tuple-element.76), channel_id=1, source_target_pairs={{0,8},{8,0},{1,9},{9,1},{2,10},{10,2},{3,11},{11,3},{4,12},{12,4},... | collective-permute-start | bytes 2506760 | tf_op jit(solution)/shard_map/ppermute | solution.py:336
  41.1 21.8 %copy-start.28 = (bf16[72,3072]{1,0:T(8,128)(2,1)}, bf16[72,3072]{1,0:T(8,128)(2,1)S(1)}, u32[]{:S(2)}) copy-start(bf16[72,3072]{1,0:T(8,128)(2,1)S(1)} %collective-permute-done.8.refs_4_) | copy-start | bytes 1327108
  41.1 11.6 %collective-permute-start.10 = (bf16[72,3072]{1,0:T(8,128)(2,1)S(1)}, bf16[72,3072]{1,0:T(8,128)(2,1)S(1)}, u32[]{:S(2)}, u32[]{:S(2)}) collective-permute-start(bf16[72,3072]{1,0:T(8,128)(2,1)S(1)} %collective-permute-done.8.refs_4_), channel_id=1, source_target_pairs={{0,6},{2,0},{4,2},{6,4},{1,7},{3,1},{5,3},{7,5},{8,14},{10,8},{12,... | collective-permute-start | bytes 1327112 | tf_op jit(solution)/shard_map/ppermute | solution.py:336
  42.9 9.8 %collective-permute-start.9 = (bf16[64,3072]{1,0:T(8,128)(2,1)}, bf16[64,3072]{1,0:T(8,128)(2,1)}, u32[]{:S(2)}, u32[]{:S(2)}) collective-permute-start(bf16[64,3072]{1,0:T(8,128)(2,1)} %collective-permute-done.6.refs_2_), channel_id=1, source_target_pairs={{0,2},{2,4},{4,6},{6,0},{1,3},{3,5},{5,7},{7,1},{8,10},{10,12},{12... | collective-permute-start | bytes 1179656 | tf_op jit(solution)/shard_map/ppermute | solution.py:336
  42.9 20.1 %collective-permute-start.5 = (bf16[72,3072]{1,0:T(8,128)(2,1)S(1)}, bf16[72,3072]{1,0:T(8,128)(2,1)}, u32[]{:S(2)}, u32[]{:S(2)}) collective-permute-start(bf16[72,3072]{1,0:T(8,128)(2,1)S(1)} %get-tuple-element.74), channel_id=1, source_target_pairs={{0,6},{2,0},{4,2},{6,4},{1,7},{3,1},{5,3},{7,5},{8,14},{10,8},{12,... | collective-permute-start | bytes 1327112 | tf_op jit(solution)/shard_map/ppermute | solution.py:336
  45.6 17.4 %collective-permute-start.4 = (bf16[64,3072]{1,0:T(8,128)(2,1)S(1)}, bf16[64,3072]{1,0:T(8,128)(2,1)}, u32[]{:S(2)}, u32[]{:S(2)}) collective-permute-start(bf16[64,3072]{1,0:T(8,128)(2,1)S(1)} %get-tuple-element.73), channel_id=1, source_target_pairs={{0,2},{2,4},{4,6},{6,0},{1,3},{3,5},{5,7},{7,1},{8,10},{10,12},{12... | collective-permute-start | bytes 1179656 | tf_op jit(solution)/shard_map/ppermute | solution.py:336
  46.3 29.0 %copy-start.34 = (s32[16]{0:T(128)}, s32[16]{0:T(128)S(1)}, u32[]{:S(2)}) copy-start(s32[16]{0:T(128)S(1)} %stack.76.order_ref) | copy-start | bytes 196
  53.5 21.9 %all-to-all-start = ((bf16[16,136,128]{2,1,0:T(8,128)(2,1)}), bf16[16,136,128]{2,1,0:T(8,128)(2,1)S(1)}, u32[]{:S(2)}, u32[]{:S(2)}) async-start(bf16[16,136,128]{2,1,0:T(8,128)(2,1)} %shard_map.155), calls=%async_computation | async-start | bytes 1114112 | tf_op jit(solution)/shard_map/all_to_all | solution.py:412
  71.7 3.1 %collective-permute-start.11 = (bf16[544,384]{1,0:T(8,128)(2,1)}, bf16[544,384]{1,0:T(8,128)(2,1)S(1)}, u32[]{:S(2)}, u32[]{:S(2)}) collective-permute-start(bf16[544,384]{1,0:T(8,128)(2,1)} %get-tuple-element.82), channel_id=1, source_target_pairs={{0,1},{1,0},{2,3},{3,2},{4,5},{5,4},{6,7},{7,6},{8,9},{9,8},{10,11... | collective-permute-start | bytes 1253384 | tf_op jit(solution)/shard_map/ppermute | solution.py:336
  73.2 2.2 %collective-permute-start.12 = (bf16[544,384]{1,0:T(8,128)(2,1)}, bf16[544,384]{1,0:T(8,128)(2,1)S(1)}, u32[]{:S(2)}, u32[]{:S(2)}) collective-permute-start(bf16[544,384]{1,0:T(8,128)(2,1)} %get-tuple-element.83), channel_id=1, source_target_pairs={{0,1},{1,0},{2,3},{3,2},{4,5},{5,4},{6,7},{7,6},{8,9},{9,8},{10,11... | collective-permute-start | bytes 1253384 | tf_op jit(solution)/shard_map/ppermute | solution.py:336
  98.4 5.5 %collective-permute-start.13 = (bf16[1088,384]{1,0:T(8,128)(2,1)}, bf16[1088,384]{1,0:T(8,128)(2,1)S(1)}, u32[]{:S(2)}, u32[]{:S(2)}) collective-permute-start(bf16[1088,384]{1,0:T(8,128)(2,1)} %get-tuple-element.87), channel_id=1, source_target_pairs={{0,1},{1,0},{2,3},{3,2},{4,5},{5,4},{6,7},{7,6},{8,9},{9,8},{10,11... | collective-permute-start | bytes 2506760 | tf_op jit(solution)/shard_map/ppermute | solution.py:336
  99.3 35.7 %all-to-all-start.1 = ((bf16[16,144,128]{2,1,0:T(8,128)(2,1)}), bf16[16,144,128]{2,1,0:T(8,128)(2,1)S(1)}, u32[]{:S(2)}, u32[]{:S(2)}) async-start(bf16[16,144,128]{2,1,0:T(8,128)(2,1)} %get-tuple-element.85), calls=%async_computation.1 | async-start | bytes 1179648 | tf_op jit(solution)/shard_map/all_to_all | solution.py:454
  111.2 41.1 %collective-permute-start.21 = (bf16[136,3072]{1,0:T(8,128)(2,1)}, bf16[136,3072]{1,0:T(8,128)(2,1)}, u32[]{:S(2)}, u32[]{:S(2)}) collective-permute-start(bf16[136,3072]{1,0:T(8,128)(2,1)} %get-tuple-element.88), channel_id=1, source_target_pairs={{0,8},{8,0},{1,9},{9,1},{2,10},{10,2},{3,11},{11,3},{4,12},{12,4},... | collective-permute-start | bytes 2506760 | tf_op jit(solution)/shard_map/ppermute | solution.py:336
  112.7 17.5 %collective-permute-start.15 = (bf16[64,3072]{1,0:T(8,128)(2,1)}, bf16[64,3072]{1,0:T(8,128)(2,1)S(1)}, u32[]{:S(2)}, u32[]{:S(2)}) collective-permute-start(bf16[64,3072]{1,0:T(8,128)(2,1)} %get-tuple-element.97), channel_id=1, source_target_pairs={{0,6},{2,0},{4,2},{6,4},{1,7},{3,1},{5,3},{7,5},{8,14},{10,8},{12,... | collective-permute-start | bytes 1179656 | tf_op jit(solution)/shard_map/ppermute | solution.py:336
  115.1 15.1 %collective-permute-start.16 = (bf16[72,3072]{1,0:T(8,128)(2,1)}, bf16[72,3072]{1,0:T(8,128)(2,1)S(1)}, u32[]{:S(2)}, u32[]{:S(2)}) collective-permute-start(bf16[72,3072]{1,0:T(8,128)(2,1)} %get-tuple-element.98), channel_id=1, source_target_pairs={{0,2},{2,4},{4,6},{6,0},{1,3},{3,5},{5,7},{7,1},{8,10},{10,12},{12... | collective-permute-start | bytes 1327112 | tf_op jit(solution)/shard_map/ppermute | solution.py:336
  115.1 15.1 %copy-start.22 = (bf16[144,3072]{1,0:T(8,128)(2,1)S(1)}, bf16[144,3072]{1,0:T(8,128)(2,1)}, u32[]{:S(2)}) copy-start(bf16[144,3072]{1,0:T(8,128)(2,1)} %get-tuple-element.96.two_ref) | copy-start | bytes 2654212
  115.1 15.1 %copy-start.23 = (bf16[128,3072]{1,0:T(8,128)(2,1)S(1)}, bf16[128,3072]{1,0:T(8,128)(2,1)}, u32[]{:S(2)}) copy-start(bf16[128,3072]{1,0:T(8,128)(2,1)} %get-tuple-element.95.one_ref) | copy-start | bytes 2359300
  129.3 5.8 %collective-permute-start.14 = (bf16[4,2,3,384,128]{4,3,2,1,0:T(8,128)(2,1)}, bf16[4,2,3,384,128]{4,3,2,1,0:T(8,128)(2,1)}, u32[]{:S(2)}, u32[]{:S(2)}) collective-permute-start(bf16[4,2,3,384,128]{4,3,2,1,0:T(8,128)(2,1)} %get-tuple-element.93), channel_id=1, source_target_pairs={{0,1},{1,0},{2,3},{3,2},{4,5},{5,4},{6,7},{7,6},{8,9},{9,8},{10,11... | collective-permute-start | bytes 7077896 | tf_op jit(solution)/shard_map/ppermute | solution.py:336
  132.1 20.2 %collective-permute-start.19 = (bf16[128,3072]{1,0:T(8,128)(2,1)}, bf16[128,3072]{1,0:T(8,128)(2,1)}, u32[]{:S(2)}, u32[]{:S(2)}) collective-permute-start(bf16[128,3072]{1,0:T(8,128)(2,1)} %get-tuple-element.99), channel_id=1, source_target_pairs={{0,6},{2,0},{4,2},{6,4},{1,7},{3,1},{5,3},{7,5},{8,14},{10,8},{12,... | collective-permute-start | bytes 2359304 | tf_op jit(solution)/shard_map/ppermute | solution.py:336
  135.1 22.5 %collective-permute-start.20 = (bf16[144,3072]{1,0:T(8,128)(2,1)}, bf16[144,3072]{1,0:T(8,128)(2,1)}, u32[]{:S(2)}, u32[]{:S(2)}) collective-permute-start(bf16[144,3072]{1,0:T(8,128)(2,1)} %get-tuple-element.100), channel_id=1, source_target_pairs={{0,2},{2,4},{4,6},{6,0},{1,3},{3,5},{5,7},{7,1},{8,10},{10,12},{12... | collective-permute-start | bytes 2654216 | tf_op jit(solution)/shard_map/ppermute | solution.py:336
  136.5 11.9 %collective-permute-start.18 = (bf16[1160,128]{1,0:T(8,128)(2,1)S(1)}, bf16[1160,128]{1,0:T(8,128)(2,1)S(1)}, u32[]{:S(2)}, u32[]{:S(2)}) collective-permute-start(bf16[1160,128]{1,0:T(8,128)(2,1)S(1)} %get-tuple-element.102), channel_id=1, source_target_pairs={{0,48},{16,0},{32,16},{48,32},{1,49},{17,1},{33,17},{49,33},{2,50}... | collective-permute-start | bytes 890888 | tf_op jit(solution)/shard_map/ppermute | solution.py:336
  139.1 6.5 %copy-start.33 = (f32[1,3072]{1,0:T(1,128)S(1)}, f32[1,3072]{1,0:T(1,128)}, u32[]{:S(2)}) copy-start(f32[1,3072]{1,0:T(1,128)} %get-tuple-element.125) | copy-start | bytes 36868
  139.1 9.3 %collective-permute-start.17 = (bf16[1160,128]{1,0:T(8,128)(2,1)S(1)}, bf16[1160,128]{1,0:T(8,128)(2,1)S(1)}, u32[]{:S(2)}, u32[]{:S(2)}) collective-permute-start(bf16[1160,128]{1,0:T(8,128)(2,1)S(1)} %get-tuple-element.105), channel_id=1, source_target_pairs={{0,16},{16,32},{32,48},{48,0},{1,17},{17,33},{33,49},{49,1},{2,18}... | collective-permute-start | bytes 890888 | tf_op jit(solution)/shard_map/ppermute | solution.py:336
  146.3 11.3 %copy-start.11 = (bf16[136,3072]{1,0:T(8,128)(2,1)S(1)}, bf16[136,3072]{1,0:T(8,128)(2,1)}, u32[]{:S(2)}) copy-start(bf16[136,3072]{1,0:T(8,128)(2,1)} %get-tuple-element.111.y_ref) | copy-start | bytes 2506756
  146.3 11.2 %copy-start.12 = (bf16[136,3072]{1,0:T(8,128)(2,1)S(1)}, bf16[136,3072]{1,0:T(8,128)(2,1)}, u32[]{:S(2)}) copy-start(bf16[136,3072]{1,0:T(8,128)(2,1)} %get-tuple-element.112.a_ref) | copy-start | bytes 2506756
  146.3 11.2 %copy-start.13 = (bf16[136,3072]{1,0:T(8,128)(2,1)S(1)}, bf16[136,3072]{1,0:T(8,128)(2,1)}, u32[]{:S(2)}) copy-start(bf16[136,3072]{1,0:T(8,128)(2,1)} %get-tuple-element.113.b_ref) | copy-start | bytes 2506756
  150.9 30.0 %collective-permute-start.23 = (bf16[2304,128]{1,0:T(8,128)(2,1)}, bf16[2304,128]{1,0:T(8,128)(2,1)}, u32[]{:S(2)}, u32[]{:S(2)}) collective-permute-start(bf16[2304,128]{1,0:T(8,128)(2,1)} %get-tuple-element.110), channel_id=1, source_target_pairs={{0,48},{16,0},{32,16},{48,32},{1,49},{17,1},{33,17},{49,33},{2,50}... | collective-permute-start | bytes 1769480 | tf_op jit(solution)/shard_map/ppermute | solution.py:336
  151.6 29.3 %collective-permute-start.22 = (bf16[2312,128]{1,0:T(8,128)(2,1)}, bf16[2312,128]{1,0:T(8,128)(2,1)}, u32[]{:S(2)}, u32[]{:S(2)}) collective-permute-start(bf16[2312,128]{1,0:T(8,128)(2,1)} %get-tuple-element.109), channel_id=1, source_target_pairs={{0,16},{16,32},{32,48},{48,0},{1,17},{17,33},{33,49},{49,1},{2,18}... | collective-permute-start | bytes 1775624 | tf_op jit(solution)/shard_map/ppermute | solution.py:336
  161.7 24.5 %collective-permute-start.26 = (bf16[136,3072]{1,0:T(8,128)(2,1)}, bf16[136,3072]{1,0:T(8,128)(2,1)S(1)}, u32[]{:S(2)}, u32[]{:S(2)}) collective-permute-start(bf16[136,3072]{1,0:T(8,128)(2,1)} %get-tuple-element.114), channel_id=1, source_target_pairs={{0,8},{8,0},{1,9},{9,1},{2,10},{10,2},{3,11},{11,3},{4,12},{12,4},... | collective-permute-start | bytes 2506760 | tf_op jit(solution)/shard_map/ppermute | solution.py:336
  162.0 24.2 %collective-permute-start.24 = (bf16[136,3072]{1,0:T(8,128)(2,1)}, bf16[136,3072]{1,0:T(8,128)(2,1)}, u32[]{:S(2)}, u32[]{:S(2)}) collective-permute-start(bf16[136,3072]{1,0:T(8,128)(2,1)} %get-tuple-element.121), channel_id=1, source_target_pairs={{0,6},{2,0},{4,2},{6,4},{1,7},{3,1},{5,3},{7,5},{8,14},{10,8},{12,... | collective-permute-start | bytes 2506760 | tf_op jit(solution)/shard_map/ppermute | solution.py:336
  162.0 24.2 %collective-permute-start.25 = (bf16[136,3072]{1,0:T(8,128)(2,1)}, bf16[136,3072]{1,0:T(8,128)(2,1)}, u32[]{:S(2)}, u32[]{:S(2)}) collective-permute-start(bf16[136,3072]{1,0:T(8,128)(2,1)} %get-tuple-element.122), channel_id=1, source_target_pairs={{0,2},{2,4},{4,6},{6,0},{1,3},{3,5},{5,7},{7,1},{8,10},{10,12},{12... | collective-permute-start | bytes 2506760 | tf_op jit(solution)/shard_map/ppermute | solution.py:336
  174.9 15.2 %all-to-all-start.2 = ((bf16[16,3,3072]{2,1,0:T(4,128)(2,1)}), bf16[16,3,3072]{2,1,0:T(4,128)(2,1)}, u32[]{:S(2)}, u32[]{:S(2)}) async-start(bf16[16,3,3072]{2,1,0:T(4,128)(2,1)} %broadcast_in_dim.46), calls=%async_computation.2 | async-start | bytes 786432 | tf_op jit(solution)/shard_map/all_to_all | solution.py:582
  180.8 5.3 %copy-start.6 = (bf16[1,128,3072]{2,1,0:T(8,128)(2,1)S(1)}, bf16[1,128,3072]{2,1,0:T(8,128)(2,1)}, u32[]{:S(2)}) copy-start(bf16[1,128,3072]{2,1,0:T(8,128)(2,1)} %param.18) | copy-start | bytes 2359300
  180.9 5.3 %copy-start.8 = (bf16[1,128,3072]{2,1,0:T(8,128)(2,1)S(1)}, bf16[1,128,3072]{2,1,0:T(8,128)(2,1)}, u32[]{:S(2)}) copy-start(bf16[1,128,3072]{2,1,0:T(8,128)(2,1)} %param.10) | copy-start | bytes 2359300
  183.6 12.1 %copy-start.16 = (f32[1152,128]{1,0:T(8,128)S(1)}, f32[1152,128]{1,0:T(8,128)}, u32[]{:S(2)}) copy-start(f32[1152,128]{1,0:T(8,128)} %copy-done.15) | copy-start | bytes 1769476
  183.6 11.5 %collective-permute-start.27 = (bf16[1160,128]{1,0:T(8,128)(2,1)S(1)}, bf16[1160,128]{1,0:T(8,128)(2,1)S(1)}, u32[]{:S(2)}, u32[]{:S(2)}) collective-permute-start(bf16[1160,128]{1,0:T(8,128)(2,1)S(1)} %get-tuple-element.119), channel_id=1, source_target_pairs={{0,64},{64,0},{1,65},{65,1},{2,66},{66,2},{3,67},{67,3},{4,68},{68... | collective-permute-start | bytes 890888 | tf_op jit(solution)/shard_map/ppermute | solution.py:336
  (18 other events, 40.5 us)
